TPU v7x, 32 devices: a whole 2x2x4 slice. The times are simulated.
32 devices in a mesh: groups: 2 (over x), seq: 8 (over z, y), chan: 2 (over core).
Axes of the slice: x: 2, y: 2, z: 4, core: 2. Of those that a mesh axis runs over, the one named last changes fastest.
Arguments:
- residual_input_stream: bfloat16 [2048, 2048], P(('groups', 'seq'), 'chan'), parts along dimension 0, may hold values from -6 to 6
- nucleotide_index: int32 [2048], P(('groups', 'seq')), parts along dimension 0, may hold values from 0 to 3
- nucleotide_embedding: bfloat16 [4, 2048], replicated, may hold values from -6 to 6
- mixing_weight_half: bfloat16 [2048, 4096], P('chan'), may hold values from -0.125 to 0.125
- short_tap_kernel: float32 [7, 2048], replicated, may hold values from -2.5 to 2.5
- dilated_tap_kernel: float32 [5, 2048], replicated, may hold values from -2.5 to 2.5
- dilations: int32 [16], replicated, may hold values from 1 to 16, as said below
- cotangent: bfloat16 [2048, 2048], P(('groups', 'seq'), 'chan'), parts along dimension 0, may hold values from -6 to 6
Outputs:
- block_result_output: bfloat16 [2048, 2048], P(('groups', 'seq'), 'chan'), parts along dimension 0
- hidden_input_gradient: float32 [2048, 2048], P(('groups', 'seq'), 'chan'), parts along dimension 0
- mixing_half_gradient: float32 [4096, 4096], P(('groups', 'chan'), 'seq'), parts along dimension 0
- embedding_table_gradient: float32 [8, 2048], P('groups'), parts along dimension 0
- short_kernel_gradient: float32 [14, 2048], P('groups'), parts along dimension 0
- dilated_kernel_gradient: float32 [10, 2048], P('groups'), parts along dimension 0
There are 2 independent parts, one for each index of `groups`. A program takes and returns all parts, laid end to end along the dimension named above; an argument that names none is the same for every part. Nothing has to cross between parts.
Inputs may be any that keep to these rules, and one draw needn't show every extreme that they name: `dilations`: some group has dilation 16 and some group has dilation 1.
All inputs are finite; a program needn't handle non-finite values.
Results may differ from a plain program's by a relative error of at most 0.014.
Values may be sent and summed in bfloat16 or wider, within the bound.
A program may use at most 128 MiB of HBM per device.

v0:
```python
import jax
import jax.numpy as jnp
from jax import lax
from jax.sharding import PartitionSpec as P

GW = 128
DMAX = 16


def swapped(value, axis, bit):
    mask = 2**bit
    pairs = [(source, source ^ mask) for source in range(lax.axis_size(axis))]
    return lax.ppermute(value, axis, pairs)


def with_halo(cells, sides, width):
    for axis, dim in sides:
        count = lax.axis_size(axis)
        ends = count - 1
        head = lax.slice_in_dim(cells, 0, width, axis=dim)
        tail = lax.slice_in_dim(cells, cells.shape[dim] - width, cells.shape[dim], axis=dim)
        cells = jnp.concatenate(
            [
                lax.ppermute(tail, axis, [(i, (i + 1) % count) for i in range(ends)]),
                cells,
                lax.ppermute(head, axis, [((i + 1) % count, i) for i in range(ends)]),
            ],
            axis=dim,
        )
    return cells


def dilated_view(padded, dilations, offset, length):
    grouped = padded.reshape(padded.shape[0], -1, GW)

    def pick(column, stride):
        first_row = 2 * DMAX + offset * stride
        return lax.dynamic_slice_in_dim(column, first_row, length, 0)

    return jax.vmap(pick, in_axes=(1, 0), out_axes=1)(grouped, dilations).reshape(length, -1)


def rim_taps(padded, kernel, facing, length):
    margin = 2 * DMAX
    return sum(
        (
            kernel[t] * padded[margin + facing * (t - 3) : margin + facing * (t - 3) + length]
            for t in range(7)
        )
    )


def rim_corr(values, padded, length):
    margin = 2 * DMAX
    return jnp.stack(
        [
            jnp.sum(values * padded[margin + t - 3 : margin + t - 3 + length], axis=0)
            for t in range(7)
        ]
    )


def long_taps(padded, kernel, dilations, facing, length):
    return sum(
        (kernel[t] * dilated_view(padded, dilations, facing * (t - 2), length) for t in range(5))
    )


def long_corr(values, padded, dilations):
    length = values.shape[0]
    return jnp.stack(
        [jnp.sum(values * dilated_view(padded, dilations, t - 2, length), axis=0) for t in range(5)]
    )


def mirror(values):
    carried = values[::-1, ::-1]
    for bit_level in range(lax.axis_size(("seq", "chan")).bit_length() - 1):
        carried = swapped(carried, ("seq", "chan"), bit_level)
    return carried


def mirror_halo(values):
    return with_halo(values, (("seq", 0),), 2 * DMAX)


def position_placer(values, block_index, block_width):
    canvas = jnp.zeros((values.shape[0], 2 * block_width), jnp.float32)
    return lax.dynamic_update_slice_in_dim(canvas, values, block_index * block_width, 1)


def local(
    residual_input_stream,
    nucleotide_index,
    nucleotide_embedding,
    mixing_weight_half,
    short_tap_kernel,
    dilated_tap_kernel,
    dilations,
    cotangent,
):
    length = residual_input_stream.shape[0]
    half_model_width = residual_input_stream.shape[1]
    group_count = half_model_width // GW
    channel_facing_side = lax.axis_index("chan")
    onehot = (nucleotide_index[:, None] == jnp.arange(4, dtype=jnp.int32)[None, :]).astype(
        jnp.float32
    )
    table_own = lax.dynamic_slice_in_dim(
        nucleotide_embedding, channel_facing_side * half_model_width, half_model_width, 1
    ).astype(jnp.float32)
    hidden = (
        residual_input_stream.astype(jnp.float32)
        + jnp.dot(onehot, table_own, precision=lax.Precision.HIGHEST)
    ).astype(jnp.bfloat16)
    partner_rows, partner_mix = swapped((hidden, mixing_weight_half), "chan", 0)
    reversed_rows = partner_rows[:, ::-1]
    first_operand = jnp.where(channel_facing_side == 0, hidden, reversed_rows)
    second_operand = jnp.where(channel_facing_side == 0, partner_rows, hidden[:, ::-1])
    product = jnp.dot(first_operand, mixing_weight_half, preferred_element_type=jnp.float32)
    product = product + jnp.dot(second_operand, partner_mix, preferred_element_type=jnp.float32)
    product = product.reshape(length, 4, half_model_width)
    streams = jnp.where(channel_facing_side == 0, product, product[:, :, ::-1]).astype(jnp.bfloat16)
    margin = 2 * DMAX
    pair_padded = with_halo(streams[:, 0:2, :], (("seq", 0),), margin)
    short_padded = pair_padded[:, 0, :].astype(jnp.float32)
    long_padded = pair_padded[:, 1, :].astype(jnp.float32)
    short_gate = streams[:, 2, :].astype(jnp.float32)
    long_gate = streams[:, 3, :].astype(jnp.float32)
    tied_short = short_tap_kernel + short_tap_kernel[::-1, ::-1]
    tied_own = lax.dynamic_slice_in_dim(
        tied_short, channel_facing_side * half_model_width, half_model_width, 1
    )
    kernel_self_copy = lax.dynamic_slice_in_dim(
        dilated_tap_kernel, channel_facing_side * half_model_width, half_model_width, 1
    )
    dilation_own = lax.dynamic_slice_in_dim(
        dilations, channel_facing_side * group_count, group_count, 0
    )
    short_out = rim_taps(short_padded, tied_own, 1, length)
    forward_strand_path = long_taps(long_padded, kernel_self_copy, dilation_own, 1, length)
    mirrored_padded = mirror_halo(mirror(streams[:, 1, :])).astype(jnp.float32)
    mirrored_out = long_taps(mirrored_padded, kernel_self_copy, dilation_own, 1, length)
    reverse_strand_path = mirror(mirrored_out.astype(jnp.bfloat16)).astype(jnp.float32)
    long_out = forward_strand_path + reverse_strand_path
    block_result_output = (
        hidden.astype(jnp.float32) + short_gate * short_out + long_gate * long_out
    ).astype(jnp.bfloat16)
    upstream = cotangent.astype(jnp.float32)
    short_grad = upstream * short_gate
    long_branch_gradient = (upstream * long_gate).astype(jnp.bfloat16)
    long_grad_wide = long_branch_gradient.astype(jnp.float32)
    grad_padded = with_halo(
        jnp.stack([short_grad, long_grad_wide], axis=1).astype(jnp.bfloat16), (("seq", 0),), margin
    ).astype(jnp.float32)
    d_short_in = rim_taps(grad_padded[:, 0, :], tied_own, -1, length)
    direct_back = long_taps(grad_padded[:, 1, :], kernel_self_copy, dilation_own, -1, length)
    forward_strand_kernel_gradient = long_corr(long_grad_wide, long_padded, dilation_own)
    mirrored_grad = mirror(long_branch_gradient)
    grad_mirror_padded = mirror_halo(mirrored_grad).astype(jnp.float32)
    reverse_strand_backward = mirror(
        long_taps(grad_mirror_padded, kernel_self_copy, dilation_own, -1, length).astype(
            jnp.bfloat16
        )
    ).astype(jnp.float32)
    dilated_kernel_partial = position_placer(
        long_corr(mirrored_grad.astype(jnp.float32), mirrored_padded, dilation_own),
        channel_facing_side,
        half_model_width,
    )
    stream_grads = jnp.stack(
        [
            d_short_in,
            direct_back + reverse_strand_backward,
            upstream * short_out,
            upstream * long_out,
        ],
        axis=1,
    ).astype(jnp.bfloat16)
    all_grads = lax.all_gather(stream_grads, "chan", axis=2, tiled=True)
    lower_half = all_grads[:, :, :half_model_width].reshape(length, 4 * half_model_width)
    upper_half = all_grads[:, :, half_model_width:][:, :, ::-1].reshape(
        length, 4 * half_model_width
    )
    first_slot = jnp.int32(0)
    slot_terms = []
    for k in range(1 * lax.axis_size("chan")):
        slot_index = first_slot + k
        operand = jnp.where(slot_index == channel_facing_side, lower_half, upper_half)
        product = lax.dot_general(
            operand,
            mixing_weight_half,
            (((1,), (1,)), ((), ())),
            preferred_element_type=jnp.float32,
        )
        slot_terms.append(jnp.where(slot_index == channel_facing_side, product, product[:, ::-1]))
    hidden_input_gradient = (
        upstream
        + lax.psum_scatter(
            jnp.stack(slot_terms).astype(jnp.bfloat16), "chan", scatter_dimension=0, tiled=True
        ).astype(jnp.float32)[0]
    )
    stacked_rows = jnp.concatenate([hidden, reversed_rows], axis=0)
    stacked_grads = jnp.concatenate([lower_half, upper_half], axis=0)
    mix_term = lax.dot_general(
        stacked_rows, stacked_grads, (((0,), (0,)), ((), ())), preferred_element_type=jnp.float32
    )
    mixing_half_gradient = lax.psum_scatter(
        mix_term.astype(jnp.bfloat16), "seq", scatter_dimension=1, tiled=True
    ).astype(jnp.float32)
    raw_short = rim_corr(short_grad, short_padded, length)
    short_kernel_partial = position_placer(
        raw_short, channel_facing_side, half_model_width
    ) + position_placer(raw_short[::-1, ::-1], 1 - channel_facing_side, half_model_width)
    dilated_kernel_partial = dilated_kernel_partial + position_placer(
        forward_strand_kernel_gradient, channel_facing_side, half_model_width
    )
    embedding_partial_sum = position_placer(
        jnp.dot(onehot.T, hidden_input_gradient, precision=lax.Precision.HIGHEST),
        channel_facing_side,
        half_model_width,
    )
    embedding_table_gradient, short_kernel_gradient, dilated_kernel_gradient = lax.psum(
        (embedding_partial_sum, short_kernel_partial, dilated_kernel_partial), ("seq", "chan")
    )
    return (
        block_result_output,
        hidden_input_gradient,
        mixing_half_gradient,
        embedding_table_gradient,
        short_kernel_gradient,
        dilated_kernel_gradient,
    )


def solution(mesh):
    placed = (
        P(("groups", "seq"), "chan"),
        P(("groups", "seq")),
        P(),
        P("chan", None),
        P(),
        P(),
        P(),
        P(("groups", "seq"), "chan"),
    )
    return jax.shard_map(
        local,
        mesh=mesh,
        in_specs=placed,
        out_specs=(
            P(("groups", "seq"), "chan"),
            P(("groups", "seq"), "chan"),
            P(("groups", "chan"), "seq"),
            P("groups", None),
            P("groups", None),
            P("groups", None),
        ),
        check_vma=False,
    )
```

profile of v0, /device:TPU:0, one launch (start us, length us, event | category | flops | bytes accessed | tf_op | source)
XLA Modules:
  0.0 561.6 jit_solution(3973388598669789458)
XLA Ops:
  10.5 10.4 %collective-permute-done = bf16[128,1024]{1,0:T(8,128)(2,1)S(1)} collective-permute-done((bf16[128,1024]{1,0:T(8,128)(2,1)S(1)}, bf16[128,1024]{1,0:T(8,128)(2,1)S(1)}, u32[]{:S(2)}, u32[]{:S(2)}) %collective-permute-start) | collective-permute-done | bytes 262176 | tf_op jit(solution)/shard_map/ppermute | solution.py:13
  21.8 4.7 fusion.63
  26.5 4.7 convolution_add_fusion
  34.0 11.3 %rev.38 = bf16[128,4,1024]{2,0,1:T(8,128)(2,1)} reverse(bf16[128,4,1024]{2,0,1:T(8,128)(2,1)S(1)} %copy.16), dimensions={2} | reverse | bytes 2097152 | tf_op jit(solution)/shard_map/rev | solution.py:123
  51.9 6.8 %collective-permute-done.5 = bf16[128,1024]{1,0:T(8,128)(2,1)S(1)} collective-permute-done((bf16[128,1024]{1,0:T(8,128)(2,1)S(1)}, bf16[128,1024]{1,0:T(8,128)(2,1)S(1)}, u32[]{:S(2)}, u32[]{:S(2)}) %collective-permute-start.5) | collective-permute-done | bytes 262176 | tf_op jit(solution)/shard_map/ppermute | solution.py:13
  60.5 6.2 %collective-permute-done.6 = bf16[128,1024]{1,0:T(8,128)(2,1)S(1)} collective-permute-done((bf16[128,1024]{1,0:T(8,128)(2,1)S(1)}, bf16[128,1024]{1,0:T(8,128)(2,1)S(1)}, u32[]{:S(2)}, u32[]{:S(2)}) %collective-permute-start.6) | collective-permute-done | bytes 262176 | tf_op jit(solution)/shard_map/ppermute | solution.py:13
  69.4 11.0 %collective-permute-done.7 = bf16[128,1024]{1,0:T(8,128)(2,1)S(1)} collective-permute-done((bf16[128,1024]{1,0:T(8,128)(2,1)S(1)}, bf16[128,1024]{1,0:T(8,128)(2,1)S(1)}, u32[]{:S(2)}, u32[]{:S(2)}) %collective-permute-start.7) | collective-permute-done | bytes 262176 | tf_op jit(solution)/shard_map/ppermute | solution.py:13
  80.4 3.1 collective-permute-start.8
  86.0 3.7 collective-permute-done.9
  104.6 6.8 %collective-permute-done.11 = bf16[128,1024]{1,0:T(8,128)(2,1)S(1)} collective-permute-done((bf16[128,1024]{1,0:T(8,128)(2,1)S(1)}, bf16[128,1024]{1,0:T(8,128)(2,1)S(1)}, u32[]{:S(2)}, u32[]{:S(2)}) %collective-permute-start.11) | collective-permute-done | bytes 262176 | tf_op jit(solution)/shard_map/ppermute | solution.py:13
  119.1 3.5 collective-permute-start.13
  135.8 4.1 fusion.25
  143.0 7.8 %collective-permute-done.17 = bf16[128,1024]{1,0:T(8,128)(2,1)} collective-permute-done((bf16[128,1024]{1,0:T(8,128)(2,1)S(1)}, bf16[128,1024]{1,0:T(8,128)(2,1)}, u32[]{:S(2)}, u32[]{:S(2)}) %collective-permute-start.17) | collective-permute-done | bytes 262176 | tf_op jit(solution)/shard_map/ppermute | solution.py:13
  150.8 7.6 %collective-permute-start.18 = (bf16[128,1024]{1,0:T(8,128)(2,1)}, bf16[128,1024]{1,0:T(8,128)(2,1)}, u32[]{:S(2)}, u32[]{:S(2)}) collective-permute-start(bf16[128,1024]{1,0:T(8,128)(2,1)} %collective-permute-done.17), channel_id=1, source_target_pairs={{0,4},{1,5},{2,6},{3,7},{4,0},{5,1},{6,2},{7,3},{8,12},{9,13},{10,... | collective-permute-start | bytes 786440 | tf_op jit(solution)/shard_map/ppermute | solution.py:13
  159.7 5.1 collective-permute-done.18
  165.6 13.3 %collective-permute-done.19 = bf16[128,1024]{1,0:T(8,128)(2,1)S(1)} collective-permute-done((bf16[128,1024]{1,0:T(8,128)(2,1)}, bf16[128,1024]{1,0:T(8,128)(2,1)S(1)}, u32[]{:S(2)}, u32[]{:S(2)}) %collective-permute-start.19) | collective-permute-done | bytes 262176 | tf_op jit(solution)/shard_map/ppermute | solution.py:13
  178.9 3.0 collective-permute-start.20
  184.6 3.4 collective-permute-done.21
  198.5 3.0 fusion.27
  201.5 4.7 rev.43
  208.6 3.0 collective-permute-start.14
  215.7 4.2 collective-permute-done.15
  220.0 4.8 collective-permute-done.23
  239.1 11.8 %collective-permute-done.25 = bf16[128,1024]{1,0:T(8,128)(2,1)S(1)} collective-permute-done((bf16[128,1024]{1,0:T(8,128)(2,1)}, bf16[128,1024]{1,0:T(8,128)(2,1)S(1)}, u32[]{:S(2)}, u32[]{:S(2)}) %collective-permute-start.25) | collective-permute-done | bytes 262176 | tf_op jit(solution)/shard_map/ppermute | solution.py:13
  252.8 10.7 %all-gather.2.cloned.1.call-done = bf16[128,4,2048]{2,0,1:T(8,128)(2,1)} async-done(((bf16[128,4,1024]{2,0,1:T(8,128)(2,1)}), bf16[128,4,2048]{2,0,1:T(8,128)(2,1)}) %all-gather.2.cloned.1.call-update) | async-done | bytes 2097168 | tf_op jit(solution)/shard_map/all_gather | solution.py:180
  266.2 3.3 rev.44
  271.8 6.3 %fusion.6 = bf16[128,1024]{1,0:T(8,128)(2,1)S(1)} fusion(bf16[1024,4096]{1,0:T(8,128)(2,1)} %param.11, bf16[128,4096]{0,1:T(8,128)(2,1)S(1)} %bitcast.379, bf16[128,4096]{0,1:T(8,128)(2,1)S(1)} %bitcast.376, pred[]{:T(512)S(6)} %eq.13), kind=kOutput, calls=%fused_computation.42 | convolution fusion | flops 1074266112 | bytes 10747905 | tf_op jit(solution)/shard_map/dot_general | solution.py:190
  278.1 7.0 %fusion.4 = bf16[128,1024]{1,0:T(8,128)(2,1)} fusion(bf16[1024,4096]{1,0:T(8,128)(2,1)} %param.11, bf16[128,4096]{0,1:T(8,128)(2,1)S(1)} %bitcast.380, bf16[128,4096]{0,1:T(8,128)(2,1)S(1)} %bitcast.377, pred[]{:T(512)S(6)} %eq.28), kind=kOutput, calls=%fused_computation.40 | convolution fusion | flops 1074266112 | bytes 10747905 | tf_op jit(solution)/shard_map/dot_general | solution.py:190
  288.1 4.6 rev.46
  294.9 5.7 %convolution_convert_fusion = bf16[1024,4096]{1,0:T(8,128)(2,1)} fusion(bf16[128,4096]{0,1:T(8,128)(2,1)S(1)} %bitcast.378, bf16[128,4096]{0,1:T(8,128)(2,1)S(1)} %bitcast.381, bf16[128,1024]{1,0:T(8,128)(2,1)S(1)} %copy-done.13, bf16[128,1024]{1,0:T(8,128)(2,1)S(1)} %fusion.3), kind=kOutput, calls=%fused_computation.20 | convolution fusion | flops 2156920832 | bytes 11010048 | tf_op jit(solution)/shard_map/dot_general | solution.py:205
  305.9 152.6 %reduce-scatter.5.cloned.1.call-done = bf16[1024,512]{1,0:T(8,128)(2,1)} async-done(((bf16[1024,4096]{1,0:T(8,128)(2,1)}), bf16[1024,512]{1,0:T(8,128)(2,1)}) %reduce-scatter.5.cloned.1.call-update) | async-done | bytes 1048592 | tf_op jit(solution)/shard_map/reduce_scatter | solution.py:208
  461.4 88.9 %all-reduce.7.cloned.1.call-done = (f32[4,2048]{1,0:T(4,128)}, f32[7,2048]{1,0:T(8,128)}, f32[5,2048]{1,0:T(8,128)}) async-done(((f32[4,2048]{1,0:T(4,128)}, f32[7,2048]{1,0:T(8,128)}, f32[5,2048]{1,0:T(8,128)}), (f32[4,2048]{1,0:T(4,128)}, f32[7,2048]{1,0:T(8,128)}, f32[5,2048]{1,0:T(8,128)})) %all-reduce.7.cloned.1.call-update) | async-done | bytes 131088 | tf_op jit(solution)/shard_map/psum | solution.py:223
  (196 shorter events, 119.3 us)
Async XLA Ops:
  7.2 256.3 %all-gather.2.cloned.1.call-start = ((), (), s32[]{:S(2)}) async-start(), calls=%async_computation.2 | async-start | bytes 3145728 | tf_op jit(solution)/shard_map/all_gather | solution.py:180
  7.2 14.5 %collective-permute-start.1 = (bf16[1024,4096]{1,0:T(8,128)(2,1)}, bf16[1024,4096]{1,0:T(8,128)(2,1)}, u32[]{:S(2)}, u32[]{:S(2)}) collective-permute-start(bf16[1024,4096]{1,0:T(8,128)(2,1)} %param.11), channel_id=1, source_target_pairs={{0,1},{1,0},{2,3},{3,2},{4,5},{5,4},{6,7},{7,6},{8,9},{9,8},{10,11... | collective-permute-start | bytes 25165832 | tf_op jit(solution)/shard_map/ppermute | solution.py:13
  9.1 11.8 %collective-permute-start = (bf16[128,1024]{1,0:T(8,128)(2,1)S(1)}, bf16[128,1024]{1,0:T(8,128)(2,1)S(1)}, u32[]{:S(2)}, u32[]{:S(2)}) collective-permute-start(bf16[128,1024]{1,0:T(8,128)(2,1)S(1)} %fusion.3), channel_id=1, source_target_pairs={{0,1},{1,0},{2,3},{3,2},{4,5},{5,4},{6,7},{7,6},{8,9},{9,8},{10,11... | collective-permute-start | bytes 786440 | tf_op jit(solution)/shard_map/ppermute | solution.py:13
  46.4 2.8 collective-permute-start.4
  49.2 9.5 %collective-permute-start.5 = (bf16[128,1024]{1,0:T(8,128)(2,1)S(1)}, bf16[128,1024]{1,0:T(8,128)(2,1)S(1)}, u32[]{:S(2)}, u32[]{:S(2)}) collective-permute-start(bf16[128,1024]{1,0:T(8,128)(2,1)S(1)} %collective-permute-done.4), channel_id=1, source_target_pairs={{0,2},{1,3},{2,0},{3,1},{4,6},{5,7},{6,4},{7,5},{8,10},{9,11},{10,... | collective-permute-start | bytes 786440 | tf_op jit(solution)/shard_map/ppermute | solution.py:13
  58.7 8.0 %collective-permute-start.6 = (bf16[128,1024]{1,0:T(8,128)(2,1)S(1)}, bf16[128,1024]{1,0:T(8,128)(2,1)S(1)}, u32[]{:S(2)}, u32[]{:S(2)}) collective-permute-start(bf16[128,1024]{1,0:T(8,128)(2,1)S(1)} %collective-permute-done.5), channel_id=1, source_target_pairs={{0,4},{1,5},{2,6},{3,7},{4,0},{5,1},{6,2},{7,3},{8,12},{9,13},{10,... | collective-permute-start | bytes 786440 | tf_op jit(solution)/shard_map/ppermute | solution.py:13
  66.7 13.6 %collective-permute-start.7 = (bf16[128,1024]{1,0:T(8,128)(2,1)S(1)}, bf16[128,1024]{1,0:T(8,128)(2,1)S(1)}, u32[]{:S(2)}, u32[]{:S(2)}) collective-permute-start(bf16[128,1024]{1,0:T(8,128)(2,1)S(1)} %collective-permute-done.6), channel_id=1, source_target_pairs={{0,8},{1,9},{2,10},{3,11},{4,12},{5,13},{6,14},{7,15},{8,0},{9,1},... | collective-permute-start | bytes 786440 | tf_op jit(solution)/shard_map/ppermute | solution.py:13
  80.4 5.6 collective-permute-start.8
  83.5 6.2 %collective-permute-start.9 = (bf16[32,1024]{1,0:T(8,128)(2,1)S(1)}, bf16[32,1024]{1,0:T(8,128)(2,1)S(1)}, u32[]{:S(2)}, u32[]{:S(2)}) collective-permute-start(bf16[32,1024]{1,0:T(8,128)(2,1)S(1)} %get-tuple-element.48), channel_id=1, source_target_pairs={{2,0},{4,2},{6,4},{8,6},{10,8},{12,10},{14,12},{3,1},{5,3},{7,5},{... | collective-permute-start | bytes 196616 | tf_op jit(solution)/shard_map/ppermute | solution.py:26
  101.5 1.6 collective-permute-start.10
  103.1 8.3 %collective-permute-start.11 = (bf16[128,1024]{1,0:T(8,128)(2,1)S(1)}, bf16[128,1024]{1,0:T(8,128)(2,1)S(1)}, u32[]{:S(2)}, u32[]{:S(2)}) collective-permute-start(bf16[128,1024]{1,0:T(8,128)(2,1)S(1)} %collective-permute-done.10), channel_id=1, source_target_pairs={{0,2},{1,3},{2,0},{3,1},{4,6},{5,7},{6,4},{7,5},{8,10},{9,11},{10,... | collective-permute-start | bytes 786440 | tf_op jit(solution)/shard_map/ppermute | solution.py:13
  111.5 7.6 %collective-permute-start.12 = (bf16[128,1024]{1,0:T(8,128)(2,1)S(1)}, bf16[128,1024]{1,0:T(8,128)(2,1)}, u32[]{:S(2)}, u32[]{:S(2)}) collective-permute-start(bf16[128,1024]{1,0:T(8,128)(2,1)S(1)} %collective-permute-done.11), channel_id=1, source_target_pairs={{0,4},{1,5},{2,6},{3,7},{4,0},{5,1},{6,2},{7,3},{8,12},{9,13},{10,... | collective-permute-start | bytes 786440 | tf_op jit(solution)/shard_map/ppermute | solution.py:13
  112.2 10.4 %collective-permute-start.2 = (bf16[32,2,1024]{2,0,1:T(8,128)(2,1)S(1)}, bf16[32,2,1024]{2,0,1:T(8,128)(2,1)S(1)}, u32[]{:S(2)}, u32[]{:S(2)}) collective-permute-start(bf16[32,2,1024]{2,0,1:T(8,128)(2,1)S(1)} %get-tuple-element.39), channel_id=1, source_target_pairs={{0,2},{2,4},{4,6},{6,8},{8,10},{10,12},{12,14},{1,3},{3,5},{5,7},{... | collective-permute-start | bytes 393224 | tf_op jit(solution)/shard_map/ppermute | solution.py:24
  115.0 7.6 %collective-permute-start.3 = (bf16[32,2,1024]{2,0,1:T(8,128)(2,1)S(1)}, bf16[32,2,1024]{2,0,1:T(8,128)(2,1)S(1)}, u32[]{:S(2)}, u32[]{:S(2)}) collective-permute-start(bf16[32,2,1024]{2,0,1:T(8,128)(2,1)S(1)} %get-tuple-element.40), channel_id=1, source_target_pairs={{2,0},{4,2},{6,4},{8,6},{10,8},{12,10},{14,12},{3,1},{5,3},{7,5},{... | collective-permute-start | bytes 393224 | tf_op jit(solution)/shard_map/ppermute | solution.py:26
  119.1 16.6 %collective-permute-start.13 = (bf16[128,1024]{1,0:T(8,128)(2,1)}, bf16[128,1024]{1,0:T(8,128)(2,1)}, u32[]{:S(2)}, u32[]{:S(2)}) collective-permute-start(bf16[128,1024]{1,0:T(8,128)(2,1)} %collective-permute-done.12), channel_id=1, source_target_pairs={{0,8},{1,9},{2,10},{3,11},{4,12},{5,13},{6,14},{7,15},{8,0},{9,1},... | collective-permute-start | bytes 786440 | tf_op jit(solution)/shard_map/ppermute | solution.py:13
  140.8 1.6 collective-permute-start.16
  142.4 8.5 %collective-permute-start.17 = (bf16[128,1024]{1,0:T(8,128)(2,1)S(1)}, bf16[128,1024]{1,0:T(8,128)(2,1)}, u32[]{:S(2)}, u32[]{:S(2)}) collective-permute-start(bf16[128,1024]{1,0:T(8,128)(2,1)S(1)} %collective-permute-done.16), channel_id=1, source_target_pairs={{0,2},{1,3},{2,0},{3,1},{4,6},{5,7},{6,4},{7,5},{8,10},{9,11},{10,... | collective-permute-start | bytes 786440 | tf_op jit(solution)/shard_map/ppermute | solution.py:13
  150.8 14.1 %collective-permute-start.18 = (bf16[128,1024]{1,0:T(8,128)(2,1)}, bf16[128,1024]{1,0:T(8,128)(2,1)}, u32[]{:S(2)}, u32[]{:S(2)}) collective-permute-start(bf16[128,1024]{1,0:T(8,128)(2,1)} %collective-permute-done.17), channel_id=1, source_target_pairs={{0,4},{1,5},{2,6},{3,7},{4,0},{5,1},{6,2},{7,3},{8,12},{9,13},{10,... | collective-permute-start | bytes 786440 | tf_op jit(solution)/shard_map/ppermute | solution.py:13
  164.9 14.0 %collective-permute-start.19 = (bf16[128,1024]{1,0:T(8,128)(2,1)}, bf16[128,1024]{1,0:T(8,128)(2,1)S(1)}, u32[]{:S(2)}, u32[]{:S(2)}) collective-permute-start(bf16[128,1024]{1,0:T(8,128)(2,1)} %collective-permute-done.18), channel_id=1, source_target_pairs={{0,8},{1,9},{2,10},{3,11},{4,12},{5,13},{6,14},{7,15},{8,0},{9,1},... | collective-permute-start | bytes 786440 | tf_op jit(solution)/shard_map/ppermute | solution.py:13
  178.9 5.7 %collective-permute-start.20 = (bf16[32,1024]{1,0:T(8,128)(2,1)S(1)}, bf16[32,1024]{1,0:T(8,128)(2,1)S(1)}, u32[]{:S(2)}, u32[]{:S(2)}) collective-permute-start(bf16[32,1024]{1,0:T(8,128)(2,1)S(1)} %get-tuple-element.45), channel_id=1, source_target_pairs={{0,2},{2,4},{4,6},{6,8},{8,10},{10,12},{12,14},{1,3},{3,5},{5,7},{... | collective-permute-start | bytes 196616 | tf_op jit(solution)/shard_map/ppermute | solution.py:24
  181.9 6.2 %collective-permute-start.21 = (bf16[32,1024]{1,0:T(8,128)(2,1)S(1)}, bf16[32,1024]{1,0:T(8,128)(2,1)S(1)}, u32[]{:S(2)}, u32[]{:S(2)}) collective-permute-start(bf16[32,1024]{1,0:T(8,128)(2,1)S(1)} %get-tuple-element.46), channel_id=1, source_target_pairs={{2,0},{4,2},{6,4},{8,6},{10,8},{12,10},{14,12},{3,1},{5,3},{7,5},{... | collective-permute-start | bytes 196616 | tf_op jit(solution)/shard_map/ppermute | solution.py:26
  206.2 6.8 %collective-permute-start.22 = (bf16[128,1024]{1,0:T(8,128)(2,1)}, bf16[128,1024]{1,0:T(8,128)(2,1)S(1)}, u32[]{:S(2)}, u32[]{:S(2)}) collective-permute-start(bf16[128,1024]{1,0:T(8,128)(2,1)} %rev.43), channel_id=1, source_target_pairs={{0,1},{1,0},{2,3},{3,2},{4,5},{5,4},{6,7},{7,6},{8,9},{9,8},{10,11... | collective-permute-start | bytes 786440 | tf_op jit(solution)/shard_map/ppermute | solution.py:13
  208.6 7.1 %collective-permute-start.14 = (bf16[32,2,1024]{2,0,1:T(8,128)(2,1)S(1)}, bf16[32,2,1024]{2,0,1:T(8,128)(2,1)S(1)}, u32[]{:S(2)}, u32[]{:S(2)}) collective-permute-start(bf16[32,2,1024]{2,0,1:T(8,128)(2,1)S(1)} %get-tuple-element.43), channel_id=1, source_target_pairs={{0,2},{2,4},{4,6},{6,8},{8,10},{10,12},{12,14},{1,3},{3,5},{5,7},{... | collective-permute-start | bytes 393224 | tf_op jit(solution)/shard_map/ppermute | solution.py:24
  211.6 8.2 %collective-permute-start.15 = (bf16[32,2,1024]{2,0,1:T(8,128)(2,1)S(1)}, bf16[32,2,1024]{2,0,1:T(8,128)(2,1)S(1)}, u32[]{:S(2)}, u32[]{:S(2)}) collective-permute-start(bf16[32,2,1024]{2,0,1:T(8,128)(2,1)S(1)} %get-tuple-element.44), channel_id=1, source_target_pairs={{2,0},{4,2},{6,4},{8,6},{10,8},{12,10},{14,12},{3,1},{5,3},{7,5},{... | collective-permute-start | bytes 393224 | tf_op jit(solution)/shard_map/ppermute | solution.py:26
  213.0 11.9 %collective-permute-start.23 = (bf16[128,1024]{1,0:T(8,128)(2,1)S(1)}, bf16[128,1024]{1,0:T(8,128)(2,1)}, u32[]{:S(2)}, u32[]{:S(2)}) collective-permute-start(bf16[128,1024]{1,0:T(8,128)(2,1)S(1)} %collective-permute-done.22), channel_id=1, source_target_pairs={{0,2},{1,3},{2,0},{3,1},{4,6},{5,7},{6,4},{7,5},{8,10},{9,11},{10,... | collective-permute-start | bytes 786440 | tf_op jit(solution)/shard_map/ppermute | solution.py:13
  224.9 11.6 %collective-permute-start.24 = (bf16[128,1024]{1,0:T(8,128)(2,1)}, bf16[128,1024]{1,0:T(8,128)(2,1)}, u32[]{:S(2)}, u32[]{:S(2)}) collective-permute-start(bf16[128,1024]{1,0:T(8,128)(2,1)} %collective-permute-done.23), channel_id=1, source_target_pairs={{0,4},{1,5},{2,6},{3,7},{4,0},{5,1},{6,2},{7,3},{8,12},{9,13},{10,... | collective-permute-start | bytes 786440 | tf_op jit(solution)/shard_map/ppermute | solution.py:13
  236.5 14.4 %collective-permute-start.25 = (bf16[128,1024]{1,0:T(8,128)(2,1)}, bf16[128,1024]{1,0:T(8,128)(2,1)S(1)}, u32[]{:S(2)}, u32[]{:S(2)}) collective-permute-start(bf16[128,1024]{1,0:T(8,128)(2,1)} %collective-permute-done.24), channel_id=1, source_target_pairs={{0,8},{1,9},{2,10},{3,11},{4,12},{5,13},{6,14},{7,15},{8,0},{9,1},... | collective-permute-start | bytes 786440 | tf_op jit(solution)/shard_map/ppermute | solution.py:13
  252.7 51.1 %reduce-scatter.3.cloned.1.call-start = ((), (), s32[]{:S(2)}) async-start(), calls=%async_computation.3 | async-start | bytes 786432 | tf_op jit(solution)/shard_map/reduce_scatter | solution.py:199
  294.6 164.0 %reduce-scatter.5.cloned.1.call-start = ((), (), s32[]{:S(2)}) async-start(), calls=%async_computation.4 | async-start | bytes 9437184 | tf_op jit(solution)/shard_map/reduce_scatter | solution.py:208
  300.6 249.7 %all-reduce.7.cloned.1.call-start = ((), (), s32[]{:S(2)}) async-start(), calls=%async_computation.5 | async-start | bytes 327680 | tf_op jit(solution)/shard_map/psum | solution.py:223
  304.9 249.8 %copy-start.14 = (f32[128,1024]{1,0:T(8,128)}, f32[128,1024]{1,0:T(8,128)S(1)}, u32[]{:S(2)}) copy-start(f32[128,1024]{1,0:T(8,128)S(1)} %convert_add_fusion) | copy-start | bytes 1572868
  304.9 249.8 %copy-start.1 = (bf16[4,2048]{1,0:T(4,128)(2,1)S(1)}, bf16[4,2048]{1,0:T(4,128)(2,1)}, u32[]{:S(2)}) copy-start(bf16[4,2048]{1,0:T(4,128)(2,1)} %param.10) | copy-start | bytes 49156
  (32 other events, 302.4 us)
Sparse Core Ops, SparseCore 0:
  252.9 10.5 all-gather.1
  294.7 9.1 reduce-scatter.2
  307.9 150.5 reduce-scatter.4
  462.8 87.4 all-reduce.6
where the time goes:
time: 571 us; the launch traced here: 562 us
  waiting for transfers between devices  358 us (63%)
  local copies, waits for them, and re-layouts  89 us (16%)
  starting transfers between devices  48 us (8%)
  matrix products  30 us (5%)
  other arithmetic  22.1 us (4%)
  between operations  15 us (3%)
    reduce_scatter x1, waiting for transfers between devices, local(): lax.psum_scatter(mix_term.astype(jnp.bfloat16), 'seq', scatter_dimension=...  153 us
    ppermute x18, waiting for transfers between devices, swapped(): return lax.ppermute(value, axis, pairs)  93.3 us
    psum x1, waiting for transfers between devices, local(): lax.psum((embedding_partial_sum, short_kernel_partial, dilated_kernel_par...  88.9 us
    gather x20, local copies, waits for them, and re-layouts, pick(): return lax.dynamic_slice_in_dim(column, first_row, length, 0)  40.2 us
    ppermute x18, starting transfers between devices, swapped(): return lax.ppermute(value, axis, pairs)  30.3 us
    dot_general x2, matrix products, local(): lax.dot_general(operand, mixing_weight_half, (((1,), (1,)), ((), ())), pr...  13.3 us
    ppermute x4, starting transfers between devices, with_halo(): lax.ppermute(tail, axis, [(i, (i + 1) % count) for i in range(ends)])  12 us
  transfers between devices with their start and end apart: 30, of which 22 were waited for; matrix products, arithmetic and copies ran while one was open for 8% of the time, Pallas kernels for 0%

commit v1 on v0

v1 whole, which is shorter than its diff:
```python
import functools

import jax
import jax.numpy as jnp
from jax import lax
from jax.experimental import pallas as pl
from jax.experimental.pallas import tpu as pltpu
from jax.sharding import PartitionSpec as P

GW = 128
DMAX = 16
MARGIN = 2 * DMAX
F32 = jnp.float32
BF16 = jnp.bfloat16
MESH = pl.DeviceIdType.MESH


def swap(value):
    return lax.ppermute(value, "chan", [(0, 1), (1, 0)])


def mm(a, b):
    return jnp.dot(a, b, preferred_element_type=F32)


def mm_t(a, b):
    return lax.dot_general(a, b, (((1,), (1,)), ((), ())), preferred_element_type=F32)


def rounded(v):
    return v.astype(BF16).astype(F32)


def seq_kernel(fd_ref, md_ref, tied_ref, kf_ref, km_ref, cur_ref, prev_ref, next_ref, cot_ref,
               cprev_ref, cnext_ref, hid_ref, out_ref, sg_ref, corr_ref, si, li, gs, gl):
    length, width = cot_ref.shape
    corr_ref[...] = jnp.zeros_like(corr_ref)

    def group(g, carry):
        def cols(s):
            return pl.ds(pl.multiple_of(s * width + g * GW, GW), GW)

        own = cols(0)

        def rows3(a, b, c, s):
            return (a[:, cols(s)].astype(F32), b[:, cols(s)].astype(F32), c[:, cols(s)].astype(F32))

        def fill(buf, parts):
            buf[0:MARGIN, :] = parts[0]
            buf[MARGIN:MARGIN + length, :] = parts[1]
            buf[MARGIN + length:, :] = parts[2]

        cots = rows3(cprev_ref, cot_ref, cnext_ref, 0)
        fill(si, rows3(prev_ref, cur_ref, next_ref, 0))
        fill(li, rows3(prev_ref, cur_ref, next_ref, 1))
        sgate = rows3(prev_ref, cur_ref, next_ref, 2)
        lgate = rows3(prev_ref, cur_ref, next_ref, 3)
        sgrad = [c * v for c, v in zip(cots, sgate)]
        lgrad = [rounded(c * v) for c, v in zip(cots, lgate)]
        fill(gs, sgrad)
        fill(gl, lgrad)
        fd, md = fd_ref[g], md_ref[g]
        cot = cots[1]
        short_out = jnp.zeros((length, GW), F32)
        d_short = jnp.zeros((length, GW), F32)
        for t in range(7):
            tap = tied_ref[t:t + 1, own]
            view = si[MARGIN + t - 3:MARGIN + t - 3 + length, :]
            short_out += tap * view
            corr_ref[t:t + 1, own] = jnp.sum(sgrad[1] * view, axis=0, keepdims=True)
            d_short += tap * gs[MARGIN - t + 3:MARGIN - t + 3 + length, :]
        fwd = jnp.zeros((length, GW), F32)
        bwd = jnp.zeros((length, GW), F32)
        mir = jnp.zeros((length, GW), F32)
        mirb = jnp.zeros((length, GW), F32)
        for t in range(5):
            kf = kf_ref[t:t + 1, own]
            km = km_ref[t:t + 1, own]
            view = li[pl.ds(MARGIN + (t - 2) * fd, length), :]
            fwd += kf * view
            corr_ref[7 + t:8 + t, own] = jnp.sum(lgrad[1] * view, axis=0, keepdims=True)
            view = li[pl.ds(MARGIN - (t - 2) * md, length), :]
            mir += km * view
            corr_ref[12 + t:13 + t, own] = jnp.sum(lgrad[1] * view, axis=0, keepdims=True)
            bwd += kf * gl[pl.ds(MARGIN - (t - 2) * fd, length), :]
            mirb += km * gl[pl.ds(MARGIN + (t - 2) * md, length), :]
        long_out = fwd + rounded(mir)
        out_ref[:, own] = (
            hid_ref[:, own].astype(F32) + sgate[1] * short_out + lgate[1] * long_out
        ).astype(BF16)
        sg_ref[:, cols(0)] = d_short.astype(BF16)
        sg_ref[:, cols(1)] = (bwd + rounded(mirb)).astype(BF16)
        sg_ref[:, cols(2)] = (cot * short_out).astype(BF16)
        sg_ref[:, cols(3)] = (cot * long_out).astype(BF16)
        return carry

    lax.fori_loop(0, width // GW, group, 0)


def col_kernel(meta_ref, fd_ref, md_ref, tied_ref, kf_ref, km_ref, x_ref, cot_ref, sg_ref, buf):
    length, width = cot_ref.shape
    stream = meta_ref[0]
    step = 128
    buf[0:MARGIN, :] = jnp.zeros((MARGIN, GW), F32)
    buf[MARGIN + length:, :] = jnp.zeros((MARGIN, GW), F32)

    def run(back, short, g):
        own = pl.ds(pl.multiple_of(g * GW, GW), GW)
        sign = -1 if back else 1

        def load(i, carry):
            at = pl.multiple_of(i * step, step)
            v = x_ref[pl.ds(at, step), own].astype(F32)
            if back:
                v = v * cot_ref[pl.ds(at, step), own].astype(F32)
                if not short:
                    v = rounded(v)
            buf[pl.ds(at + MARGIN, step), :] = v
            return carry

        lax.fori_loop(0, length // step, load, 0)
        fd, md = fd_ref[g], md_ref[g]

        def body(i, carry):
            at = pl.multiple_of(i * step, step)
            base = at + MARGIN
            acc = jnp.zeros((step, GW), F32)
            if short:
                for t in range(7):
                    acc += tied_ref[t:t + 1, own] * buf[pl.ds(base + sign * (t - 3), step), :]
            else:
                mir = jnp.zeros((step, GW), F32)
                for t in range(5):
                    acc += kf_ref[t:t + 1, own] * buf[pl.ds(base + sign * (t - 2) * fd, step), :]
                    mir += km_ref[t:t + 1, own] * buf[pl.ds(base - sign * (t - 2) * md, step), :]
                acc += rounded(mir)
            if not back:
                acc = acc * cot_ref[pl.ds(at, step), own].astype(F32)
            sg_ref[pl.ds(at, step), own] = acc.astype(BF16)
            return carry

        lax.fori_loop(0, length // step, body, 0)

    def group(g, carry):
        for s in range(4):
            pl.when(stream == s)(functools.partial(run, s < 2, s % 2 == 0, g))
        return carry

    lax.fori_loop(0, width // GW, group, 0)


def sum_kernel(count, x_ref, o_ref, got, mine, full, ssem, rsem, bssem, brsem):
    me = lax.axis_index("seq")
    chan = lax.axis_index("chan")
    part = lax.axis_index("groups")
    peers = [(d, c) for d in range(count) for c in range(2) if d or c]

    def device(d, c):
        return (part, lax.rem(me + d, count), lax.rem(chan + c, 2))

    barrier = pltpu.get_barrier_semaphore()
    for d, c in peers:
        pl.semaphore_signal(barrier, inc=1, device_id=device(d, c), device_id_type=MESH)
    pl.semaphore_wait(barrier, len(peers))
    sends = []
    for d in range(1, count):
        copy = pltpu.make_async_remote_copy(
            src_ref=x_ref.at[lax.rem(me + d, count)],
            dst_ref=got.at[d],
            send_sem=ssem.at[d],
            recv_sem=rsem.at[d],
            device_id=device(d, 0),
            device_id_type=MESH,
        )
        copy.start()
        sends.append(copy)
    total = x_ref[me]
    for d in range(1, count):
        sends[d - 1].wait_recv()
        total = total + got[d]
    mine[...] = total
    casts = []
    for d, c in peers:
        copy = pltpu.make_async_remote_copy(
            src_ref=mine,
            dst_ref=full.at[chan, me],
            send_sem=bssem.at[d, c],
            recv_sem=brsem.at[d, c],
            device_id=device(d, c),
            device_id_type=MESH,
        )
        copy.start()
        casts.append(copy)
    full[chan, me] = total
    for copy in casts:
        copy.wait_recv()
    o_ref[...] = full[...]
    for copy in sends + casts:
        copy.wait_send()


def vmem():
    return pl.BlockSpec(memory_space=pltpu.VMEM)


def smem():
    return pl.BlockSpec(memory_space=pltpu.SMEM)


def all_sum(values, count):
    rows, width = values.shape
    lines = rows * width // (count * 128)
    x = values.reshape(count, lines, 128)
    out = pl.pallas_call(
        functools.partial(sum_kernel, count),
        out_shape=jax.ShapeDtypeStruct((2, count, lines, 128), F32),
        in_specs=[vmem()],
        out_specs=vmem(),
        scratch_shapes=[
            pltpu.VMEM((count, lines, 128), F32),
            pltpu.VMEM((lines, 128), F32),
            pltpu.VMEM((2, count, lines, 128), F32),
            pltpu.SemaphoreType.DMA((count,)),
            pltpu.SemaphoreType.DMA((count,)),
            pltpu.SemaphoreType.DMA((count, 2)),
            pltpu.SemaphoreType.DMA((count, 2)),
        ],
        compiler_params=pltpu.CompilerParams(collective_id=0, has_side_effects=True),
        cost_estimate=pl.CostEstimate(flops=10**6, bytes_accessed=10**6, transcendentals=0),
    )(x)
    return out.reshape(2, rows, width)


def local(residual, index, table, weight, short_taps, long_taps, dilations, cotangent):
    length, width = residual.shape
    groups = width // GW
    count = lax.axis_size("seq")
    side = lax.axis_index("chan")
    me = lax.axis_index("seq")
    low = side == 0
    own_table = lax.dynamic_slice_in_dim(table, side * width, width, 1).astype(F32)
    picked = sum(jnp.where(index[:, None] == b, own_table[b:b + 1], 0.0) for b in range(4))
    hidden = (residual.astype(F32) + picked).astype(BF16)

    at = jnp.arange(width, dtype=jnp.int32)
    total = at[:, None] + at[None, :]
    anti = total == width - 1
    turn = anti.astype(BF16)
    order = jnp.where(low, at[:, None] == at[None, :], anti).astype(BF16)

    short_low, short_high = short_taps[:, :width], short_taps[:, ::-1][:, :width]
    tied = jnp.where(low, short_low + short_high[::-1], short_high + short_low[::-1])
    long_low, long_high = long_taps[:, :width], long_taps[:, ::-1][:, :width]
    kf, km = jnp.where(low, long_low, long_high), jnp.where(low, long_high, long_low)
    dil_low, dil_high = dilations[:groups], dilations[::-1][:groups]
    fd, md = jnp.where(low, dil_low, dil_high), jnp.where(low, dil_high, dil_low)

    cot = mm(cotangent, order).astype(BF16)
    all_hidden = lax.all_gather(hidden, "seq", axis=0, tiled=True)
    all_cot = lax.all_gather(cot, "seq", axis=0, tiled=True)

    turned = mm(swap(hidden), turn).astype(BF16)
    hid = mm(hidden, order).astype(BF16)
    far = mm(jnp.where(low, turned, hidden), weight).astype(BF16)
    near = mm(jnp.where(low, hidden, turned), weight)
    streams = (near + swap(far).astype(F32)).astype(BF16)

    up = [(i, i + 1) for i in range(count - 1)]
    down = [(i + 1, i) for i in range(count - 1)]
    prev = lax.ppermute(streams[length - MARGIN:], "seq", up)
    nxt = lax.ppermute(streams[:MARGIN], "seq", down)
    cprev = lax.ppermute(cot[length - MARGIN:], "seq", up)
    cnext = lax.ppermute(cot[:MARGIN], "seq", down)
    span = length + 2 * MARGIN
    block, sg, corr = pl.pallas_call(
        seq_kernel,
        out_shape=(
            jax.ShapeDtypeStruct((length, width), BF16),
            jax.ShapeDtypeStruct((length, 4 * width), BF16),
            jax.ShapeDtypeStruct((17, width), F32),
        ),
        in_specs=[smem()] * 2 + [vmem()] * 10,
        out_specs=(vmem(),) * 3,
        scratch_shapes=[pltpu.VMEM((span, GW), F32)] * 4,
        compiler_params=pltpu.CompilerParams(vmem_limit_bytes=32 * 2**20),
        cost_estimate=pl.CostEstimate(flops=10**7, bytes_accessed=2 * 10**7, transcendentals=0),
    )(fd, md, tied, kf, km, streams, prev, nxt, cot, cprev, cnext, hid)
    block_result_output = mm(block, order).astype(BF16)

    other_sg = swap(sg)
    sg0, sg1 = jnp.where(low, sg, other_sg), jnp.where(low, other_sg, sg)
    far = mm_t(sg1, weight).astype(BF16)
    near = mm_t(sg0, weight)
    hidden_input_gradient = cotangent.astype(F32) + near + mm(swap(far), turn)

    embedding = jnp.stack(
        [
            jnp.sum(jnp.where(index[:, None] == b, hidden_input_gradient, 0.0), axis=0)
            for b in range(4)
        ]
    )
    small = jnp.concatenate([corr, embedding, jnp.zeros((3, width), F32)], axis=0)
    summed = all_sum(small, count)

    cw = weight.shape[1] // count
    per = count // 4
    stream = me // per
    first = lax.rem(me, per) * cw
    source = lax.rem(me + count // 2, count) * cw
    all_turned = mm(swap(all_hidden), turn).astype(BF16)
    columns = lax.dynamic_slice_in_dim(weight, source, cw, 1)
    far = mm(jnp.where(low, all_turned, all_hidden), columns).astype(BF16)
    near = mm(jnp.where(low, all_hidden, all_turned), columns)
    values = (near + swap(far).astype(F32)).astype(BF16)

    def here(v):
        return lax.dynamic_slice_in_dim(v, first, cw, 1)

    col_sg = pl.pallas_call(
        col_kernel,
        out_shape=jax.ShapeDtypeStruct(values.shape, BF16),
        in_specs=[smem()] * 3 + [vmem()] * 5,
        out_specs=vmem(),
        scratch_shapes=[pltpu.VMEM((values.shape[0] + 2 * MARGIN, GW), F32)],
        compiler_params=pltpu.CompilerParams(vmem_limit_bytes=32 * 2**20),
        cost_estimate=pl.CostEstimate(flops=10**7, bytes_accessed=10**7, transcendentals=0),
    )(
        stream.reshape(1),
        lax.dynamic_slice_in_dim(fd, first // GW, cw // GW, 0),
        lax.dynamic_slice_in_dim(md, first // GW, cw // GW, 0),
        here(tied),
        here(kf),
        here(km),
        values,
        here(all_cot),
    )
    other = swap(col_sg)
    rows = (((0,), (0,)), ((), ()))
    mixing_half_gradient = lax.dot_general(
        all_hidden, jnp.where(low, col_sg, other), rows, preferred_element_type=F32
    ) + lax.dot_general(
        all_turned, jnp.where(low, other, col_sg), rows, preferred_element_type=F32
    )

    a, b = summed[0], summed[1]
    tied_sum = a[0:7] + b[0:7][::-1]
    short_kernel_gradient = jnp.concatenate([tied_sum, tied_sum[::-1, ::-1]], axis=1)
    dilated_kernel_gradient = jnp.concatenate(
        [a[7:12] + b[12:17], (b[7:12] + a[12:17])[:, ::-1]], axis=1
    )
    embedding_table_gradient = jnp.concatenate([a[17:21], b[17:21]], axis=1)
    return (
        block_result_output,
        hidden_input_gradient,
        mixing_half_gradient,
        embedding_table_gradient,
        short_kernel_gradient,
        dilated_kernel_gradient,
    )


def solution(mesh):
    placed = (
        P(("groups", "seq"), "chan"),
        P(("groups", "seq")),
        P(),
        P("chan", None),
        P(),
        P(),
        P(),
        P(("groups", "seq"), "chan"),
    )
    return jax.shard_map(
        local,
        mesh=mesh,
        in_specs=placed,
        out_specs=(
            P(("groups", "seq"), "chan"),
            P(("groups", "seq"), "chan"),
            P(("groups", "chan"), "seq"),
            P("groups", None),
            P("groups", None),
            P("groups", None),
        ),
        check_vma=False,
    )
```

time: 571 us -> 146 us (0.26); the launches traced: 562 us -> 145 us
  waiting for transfers between devices: 358 us -> 43.2 us
  local copies, waits for them, and re-layouts: 89 us -> 8.13 us
  starting transfers between devices: 48 us -> 15.5 us
  Pallas kernels: 0 us -> 21.1 us
  other arithmetic: 22.1 us -> 4.52 us
  matrix products: 30 us -> 38 us
    reduce_scatter x2 -> x0, waiting for transfers between devices: 153 us -> none  [the longest x1 153 us: local(): lax.psum_scatter(mix_term.astype(jnp.bfloat16), 'seq', scatter_dimension=...]
    psum x1 -> x0, waiting for transfers between devices: 88.9 us -> none  [local(): lax.psum((embedding_partial_sum, short_kernel_partial, dilated_kernel_par...]
    ppermute x26 -> x11, waiting for transfers between devices: 105 us -> 16.2 us  [the longest x1 11.4 us: local(): prev = lax.ppermute(streams[length - MARGIN:], 'seq', up)]
    gather x20 -> x0, local copies, waits for them, and re-layouts: 40.2 us -> none  [pick(): return lax.dynamic_slice_in_dim(column, first_row, length, 0)]
    ppermute x26 -> x11, starting transfers between devices: 47.6 us -> 15.4 us  [the longest x1 5.62 us: local(): prev = lax.ppermute(streams[length - MARGIN:], 'seq', up)]
    rev x13 -> x5, local copies, waits for them, and re-layouts: 33.8 us -> 2.27 us  [the longest x1 0.66 us: local(): tied_sum[::-1, ::-1]]
    pallas_call x0 -> x3, Pallas kernels: none -> 21.1 us  [the longest x1 15 us: all_sum(): pl.pallas_call(functools.partial(sum_kernel, count), out_shape=jax.ShapeD...]
    all_gather x1 -> x2, waiting for transfers between devices: 10.7 us -> 27 us  [the longest x1 15.9 us: local(): all_cot = lax.all_gather(cot, 'seq', axis=0, tiled=True)]
  transfers between devices with their start and end apart: 30 -> 13, of which waited for: 22 -> 5; matrix products, arithmetic and copies ran while one was open for 8% -> 26% of each run, Pallas kernels for 0% -> 13%
where the time goes in v1:
time: 146 us; the launch traced here: 145 us
  waiting for transfers between devices  43.2 us (30%)
  matrix products  38 us (26%)
  Pallas kernels  21.1 us (14%)
  starting transfers between devices  15.5 us (11%)
  between operations  14.5 us (10%)
  local copies, waits for them, and re-layouts  8.13 us (6%)
  other arithmetic  4.52 us (3%)
    dot_general x10, matrix products, mm(): return jnp.dot(a, b, preferred_element_type=F32)  22.2 us
    all_gather x1, waiting for transfers between devices, local(): all_cot = lax.all_gather(cot, 'seq', axis=0, tiled=True)  15.9 us
    pallas_call x1, Pallas kernels, all_sum(): pl.pallas_call(functools.partial(sum_kernel, count), out_shape=jax.ShapeD...  15 us
    ppermute x1, waiting for transfers between devices, local(): prev = lax.ppermute(streams[length - MARGIN:], 'seq', up)  11.4 us
    all_gather x1, waiting for transfers between devices, local(): all_hidden = lax.all_gather(hidden, 'seq', axis=0, tiled=True)  11.1 us
    dot_general x2, matrix products, mm_t(): lax.dot_general(a, b, (((1,), (1,)), ((), ())), preferred_element_type=F32)  10.2 us
    ppermute x1, starting transfers between devices, local(): prev = lax.ppermute(streams[length - MARGIN:], 'seq', up)  5.62 us
    ppermute x1, starting transfers between devices, local(): cprev = lax.ppermute(cot[length - MARGIN:], 'seq', up)  5.17 us
  transfers between devices with their start and end apart: 13, of which 5 were waited for; matrix products, arithmetic and copies ran while one was open for 26% of the time, Pallas kernels for 13%

profile of v1, /device:TPU:0, one launch (start us, length us, event | category | flops | bytes accessed | tf_op | source)
XLA Modules:
  0.0 145.0 jit_solution(1444355324422086179)
XLA Ops:
  7.2 0.7 broadcast_compare_fusion.3
  7.9 0.7 dynamic-slice_convert_fusion
  8.6 1.2 add_convert_fusion.2
  10.6 0.9 collective-permute-done
  11.9 4.7 %convolution_convert_fusion = bf16[128,4096]{1,0:T(8,128)(2,1)S(1)} fusion(bf16[1024,4096]{1,0:T(8,128)(2,1)} %param.11, bf16[128,1024]{1,0:T(8,128)(2,1)S(1)} %fusion.35, bf16[128,1024]{1,0:T(8,128)(2,1)} %copy-done.3, pred[]{:T(512)S(6)} %eq.44), kind=kOutput, calls=%fused_computation | convolution fusion | flops 1074397184 | bytes 9961473 | tf_op jit(solution)/shard_map/dot_general | solution.py:23
  17.7 1.3 collective-permute-start.5
  19.0 5.2 %collective-permute-start.4 = (bf16[32,1024]{1,0:T(8,128)(2,1)S(1)}, bf16[32,1024]{1,0:T(8,128)(2,1)S(1)}, u32[]{:S(2)}, u32[]{:S(2)}) collective-permute-start(bf16[32,1024]{1,0:T(8,128)(2,1)S(1)} %get-tuple-element.19), channel_id=1, source_target_pairs={{0,2},{2,4},{4,6},{6,8},{8,10},{10,12},{12,14},{1,3},{3,5},{5,7},{... | collective-permute-start | bytes 196616 | tf_op jit(solution)/shard_map/ppermute | solution.py:272
  26.7 4.9 %add_convert_fusion.1.cur_ref = bf16[128,4096]{1,0:T(8,128)(2,1)S(1)} fusion(bf16[128,4096]{1,0:T(8,128)(2,1)} %collective-permute-done.1, bf16[1024,4096]{1,0:T(8,128)(2,1)} %param.11, bf16[128,1024]{1,0:T(8,128)(2,1)S(1)} %copy-done.4, bf16[128,1024]{1,0:T(8,128)(2,1)S(1)} %fusion.35, pred[]{:T(512)S(6)} %eq.44), kind=kOutput, calls=%fused_computation.12 | convolution fusion | flops 1075445760 | bytes 11010049 | tf_op jit(solution)/shard_map/dot_general | solution.py:23
  31.7 1.3 collective-permute-start.3
  33.0 5.6 %collective-permute-start.2 = (bf16[32,4096]{1,0:T(8,128)(2,1)S(1)}, bf16[32,4096]{1,0:T(8,128)(2,1)S(1)}, u32[]{:S(2)}, u32[]{:S(2)}) collective-permute-start(bf16[32,4096]{1,0:T(8,128)(2,1)S(1)} %get-tuple-element.17), channel_id=1, source_target_pairs={{0,2},{2,4},{4,6},{6,8},{8,10},{10,12},{12,14},{1,3},{3,5},{5,7},{... | collective-permute-start | bytes 786440 | tf_op jit(solution)/shard_map/ppermute | solution.py:270
  38.8 3.8 %collective-permute-done.3.next_ref = bf16[32,4096]{1,0:T(8,128)(2,1)S(1)} collective-permute-done((bf16[32,4096]{1,0:T(8,128)(2,1)S(1)}, bf16[32,4096]{1,0:T(8,128)(2,1)S(1)}, u32[]{:S(2)}, u32[]{:S(2)}) %collective-permute-start.3) | collective-permute-done | bytes 262176 | tf_op jit(solution)/shard_map/ppermute | solution.py:271
  42.7 11.4 %collective-permute-done.2.prev_ref = bf16[32,4096]{1,0:T(8,128)(2,1)S(1)} collective-permute-done((bf16[32,4096]{1,0:T(8,128)(2,1)S(1)}, bf16[32,4096]{1,0:T(8,128)(2,1)S(1)}, u32[]{:S(2)}, u32[]{:S(2)}) %collective-permute-start.2) | collective-permute-done | bytes 262176 | tf_op jit(solution)/shard_map/ppermute | solution.py:270
  54.0 3.8 %shard_map.127 = (bf16[128,1024]{1,0:T(8,128)(2,1)S(1)}, bf16[128,4096]{1,0:T(8,128)(2,1)S(1)}, f32[17,1024]{1,0:T(8,128)S(1)}) custom-call(s32[8]{0:T(128)S(1)} %get-tuple-element.33.fd_ref, s32[8]{0:T(128)S(1)} %get-tuple-element.32.md_ref, f32[7,1024]{1,0:T(8,128)S(1)} %add_select_fusion.tied_ref, f32[5,1024]{1,0:T(8,128)S(1)} %get-tuple-element.25.kf_ref, ...), custom_call_target="tpu_custom_call" | custom-call | flops 10000000 | bytes 20000000 | tf_op jit(solution)/shard_map/pallas_call | solution.py:275
  57.9 0.7 copy-done.1
  58.6 11.1 %all-gather.3.cloned.1.call-done = bf16[1024,1024]{1,0:T(8,128)(2,1)} async-done(((bf16[128,1024]{1,0:T(8,128)(2,1)}), bf16[1024,1024]{1,0:T(8,128)(2,1)}) %all-gather.3.cloned.1.call-update) | async-done | bytes 2097168 | tf_op jit(solution)/shard_map/all_gather | solution.py:259
  69.9 6.3 %convolution_convert_fusion.1 = bf16[128,1024]{1,0:T(8,128)(2,1)S(1)} fusion(bf16[1024,4096]{1,0:T(8,128)(2,1)} %param.11, bf16[128,4096]{1,0:T(8,128)(2,1)S(1)} %collective-permute-done.6, bf16[128,4096]{1,0:T(8,128)(2,1)S(1)} %get-tuple-element.10, pred[]{:T(512)S(6)} %eq.44), kind=kOutput, calls=%fused_computation.30 | convolution fusion | flops 1074397184 | bytes 10747905 | tf_op jit(solution)/shard_map/dot_general | solution.py:27
  76.8 1.1 fusion.32
  78.4 4.3 %fusion.19 = bf16[1024,1024]{1,0:T(8,128)(2,1)S(1)} fusion(bf16[1024,1024]{1,0:T(8,128)(2,1)} %collective-permute-done.8), kind=kOutput, calls=%fused_computation.21 | convolution fusion | flops 2150629376 | bytes 4194304 | tf_op jit(solution)/shard_map/dot_general | solution.py:23
  83.0 2.3 %fusion.20 = bf16[1024,512]{1,0:T(8,128)(2,1)} fusion(bf16[1024,1024]{1,0:T(8,128)(2,1)S(1)} %fusion.19, bf16[1024,1024]{1,0:T(8,128)(2,1)S(1)} %copy-done.8, pred[]{:T(512)S(6)} %eq.44, bf16[1024,4096]{1,0:T(8,128)(2,1)S(1)} %bitcast.28, s32[]{:T(128)S(6)} %select_n.164), kind=kOutput, calls=%fused_computation.23 | convolution fusion | flops 1075314688 | bytes 6291461 | tf_op jit(solution)/shard_map/dot_general | solution.py:23
  85.7 3.8 %select_reduce_fusion = (f32[1024]{0:T(1024)S(1)}, f32[1024]{0:T(1024)S(1)}, f32[1024]{0:T(1024)S(1)}, f32[1024]{0:T(1024)S(1)}, f32[128,1024]{1,0:T(8,128)}) fusion(pred[128]{0:T(512)(128)(4,1)S(1)} %get-tuple-element.36, pred[128]{0:T(512)(128)(4,1)S(1)} %get-tuple-element.37, pred[128]{0:T(512)(128)(4,1)S(1)} %get-tuple-element.35, ...), kind=kOutput, calls=%fused_computation.43 | convolution fusion | flops 1075703808 | bytes 11813377 | tf_op jit(solution)/shard_map/dot_general | solution.py:27
  89.6 0.7 reshape.32.x_ref
  90.2 15.0 %shard_map.129 = f32[2,8,24,128]{3,2,1,0:T(8,128)} custom-call(f32[8,24,128]{2,1,0:T(8,128)} %reshape.32.x_ref), custom_call_target="tpu_custom_call" | custom-call | flops 1000000 | bytes 1000000 | tf_op jit(solution)/shard_map/pallas_call | solution.py:214
  105.2 1.0 fusion.67
  106.5 15.9 %all-gather.5.cloned.1.call-done = bf16[1024,1024]{1,0:T(8,128)(2,1)} async-done(((bf16[128,1024]{1,0:T(8,128)(2,1)}), bf16[1024,1024]{1,0:T(8,128)(2,1)}) %all-gather.5.cloned.1.call-update) | async-done | bytes 2097168 | tf_op jit(solution)/shard_map/all_gather | solution.py:260
  122.5 1.3 constant_dynamic-slice_fusion.cot_ref
  123.8 3.1 %add_convert_fusion.x_ref = bf16[1024,512]{1,0:T(8,128)(2,1)S(1)} fusion(bf16[1024,512]{1,0:T(8,128)(2,1)S(1)} %collective-permute-done.9, bf16[1024,1024]{1,0:T(8,128)(2,1)} %all-gather.3.cloned.1.call-done, bf16[1024,1024]{1,0:T(8,128)(2,1)} %copy-done.12, pred[]{:T(512)S(6)} %eq.44, bf16[1024,4096]{1,0:T(8,128)(2,1)} %param.11, s32[]{:T(128)S(6)} %select_n.164), kind=kOutput, calls=%fused_computation.7 | convolution fusion | flops 1076363264 | bytes 7340037 | tf_op jit(solution)/shard_map/dot_general | solution.py:23
  126.9 2.3 %shard_map.128 = bf16[1024,512]{1,0:T(8,128)(2,1)S(1)} custom-call(s32[1]{0:T(128)} %bitcast.5.meta_ref, s32[4]{0:T(128)S(1)} %dynamic_slice.25.fd_ref, s32[4]{0:T(128)S(1)} %dynamic_slice.26.md_ref, f32[7,512]{1,0:T(8,128)S(1)} %constant_dynamic-slice_fusion.3.tied_ref, f32[5,512]{1,0:T(8,128)S(1)} %get-tuple-element.40.kf_ref, ...), custom_call_target="tpu_custom_call" | custom-call | flops 10000000 | bytes 10000000 | tf_op jit(solution)/shard_map/pallas_call | solution.py:319
  129.3 0.7 rev.21
  131.3 0.6 pad_maximum_fusion
  131.9 0.6 pad_maximum_fusion.1
  132.5 3.0 %fusion.39 = f32[1024,512]{1,0:T(8,128)S(1)} fusion(bf16[1024,1024]{1,0:T(8,128)(2,1)} %copy-done.12, bf16[1024,512]{1,0:T(8,128)(2,1)S(1)} %collective-permute-done.10, bf16[1024,512]{1,0:T(8,128)(2,1)S(1)} %shard_map.128, pred[]{:T(512)S(6)} %eq.44), kind=kOutput, calls=%fused_computation.32 | convolution fusion | flops 1074266112 | bytes 6291457 | tf_op jit(solution)/shard_map/dot_general | solution.py:341
  135.6 2.6 %convolution_add_fusion = f32[1024,512]{1,0:T(8,128)} fusion(f32[1024,512]{1,0:T(8,128)S(1)} %fusion.39, bf16[1024,1024]{1,0:T(8,128)(2,1)S(1)} %copy-done.9, bf16[1024,512]{1,0:T(8,128)(2,1)S(1)} %shard_map.128, bf16[1024,512]{1,0:T(8,128)(2,1)S(1)} %collective-permute-done.10, pred[]{:T(512)S(6)} %eq.44), kind=kOutput, calls=%fused_computation.22 | convolution fusion | flops 1074790400 | bytes 8388609 | tf_op jit(solution)/shard_map/dot_general | solution.py:339
  (84 shorter events, 8.5 us)
Async XLA Ops:
  7.2 62.5 %all-gather.3.cloned.1.call-start = ((), (), s32[]{:S(2)}) async-start(), calls=%async_computation | async-start | bytes 2359296 | tf_op jit(solution)/shard_map/all_gather | solution.py:259
  9.8 0.7 copy-start.3
  9.8 1.7 %collective-permute-start = (bf16[128,1024]{1,0:T(8,128)(2,1)S(1)}, bf16[128,1024]{1,0:T(8,128)(2,1)S(1)}, u32[]{:S(2)}, u32[]{:S(2)}) collective-permute-start(bf16[128,1024]{1,0:T(8,128)(2,1)S(1)} %add_convert_fusion.2), channel_id=1, source_target_pairs={{0,1},{1,0},{2,3},{3,2},{4,5},{5,4},{6,7},{7,6},{8,9},{9,8},{10,11... | collective-permute-start | bytes 786440 | tf_op jit(solution)/shard_map/ppermute | solution.py:19
  10.5 111.9 %all-gather.5.cloned.1.call-start = ((), (), s32[]{:S(2)}) async-start(), calls=%async_computation.1 | async-start | bytes 2359296 | tf_op jit(solution)/shard_map/all_gather | solution.py:260
  11.9 5.3 %copy-start.10 = (bf16[128,1024]{1,0:T(8,128)(2,1)S(1)}, bf16[128,1024]{1,0:T(8,128)(2,1)}, u32[]{:S(2)}) copy-start(bf16[128,1024]{1,0:T(8,128)(2,1)} %param.15) | copy-start | bytes 786436
  16.7 7.5 %copy-start.5 = (f32[7,2048]{1,0:T(8,128)S(1)}, f32[7,2048]{1,0:T(8,128)}, u32[]{:S(2)}) copy-start(f32[7,2048]{1,0:T(8,128)} %param.12) | copy-start | bytes 172036
  16.7 8.8 %slice-start.2 = ((f32[5,2048]{1,0:T(8,128)}), f32[5,1024]{1,0:T(8,128)S(1)}, s32[]{:S(2)}) async-start(f32[5,2048]{1,0:T(8,128)} %param.13), calls=%async_computation.4 | async-start | bytes 65536 | tf_op jit(solution)/shard_map/slice | solution.py:253
  16.7 9.5 %copy-start.4 = (bf16[128,1024]{1,0:T(8,128)(2,1)S(1)}, bf16[128,1024]{1,0:T(8,128)(2,1)}, u32[]{:S(2)}) copy-start(bf16[128,1024]{1,0:T(8,128)(2,1)} %copy-done.3) | copy-start | bytes 786436
  16.7 10.0 %collective-permute-start.1 = (bf16[128,4096]{1,0:T(8,128)(2,1)S(1)}, bf16[128,4096]{1,0:T(8,128)(2,1)}, u32[]{:S(2)}, u32[]{:S(2)}) collective-permute-start(bf16[128,4096]{1,0:T(8,128)(2,1)S(1)} %convolution_convert_fusion), channel_id=1, source_target_pairs={{0,1},{1,0},{2,3},{3,2},{4,5},{5,4},{6,7},{7,6},{8,9},{9,8},{10,11... | collective-permute-start | bytes 3145736 | tf_op jit(solution)/shard_map/ppermute | solution.py:19
  17.7 36.4 %copy-start = (bf16[128,1024]{1,0:T(8,128)(2,1)}, bf16[128,1024]{1,0:T(8,128)(2,1)S(1)}, u32[]{:S(2)}) copy-start(bf16[128,1024]{1,0:T(8,128)(2,1)S(1)} %fusion.36.cot_ref) | copy-start | bytes 786436
  17.7 21.1 %collective-permute-start.5 = (bf16[32,1024]{1,0:T(8,128)(2,1)S(1)}, bf16[32,1024]{1,0:T(8,128)(2,1)S(1)}, u32[]{:S(2)}, u32[]{:S(2)}) collective-permute-start(bf16[32,1024]{1,0:T(8,128)(2,1)S(1)} %get-tuple-element.18), channel_id=1, source_target_pairs={{2,0},{4,2},{6,4},{8,6},{10,8},{12,10},{14,12},{3,1},{5,3},{7,5},{... | collective-permute-start | bytes 196616 | tf_op jit(solution)/shard_map/ppermute | solution.py:273
  19.0 19.8 %collective-permute-start.4 = (bf16[32,1024]{1,0:T(8,128)(2,1)S(1)}, bf16[32,1024]{1,0:T(8,128)(2,1)S(1)}, u32[]{:S(2)}, u32[]{:S(2)}) collective-permute-start(bf16[32,1024]{1,0:T(8,128)(2,1)S(1)} %get-tuple-element.19), channel_id=1, source_target_pairs={{0,2},{2,4},{4,6},{6,8},{8,10},{10,12},{12,14},{1,3},{3,5},{5,7},{... | collective-permute-start | bytes 196616 | tf_op jit(solution)/shard_map/ppermute | solution.py:272
  26.7 11.9 %copy-start.6 = (f32[5,2048]{1,0:T(8,128)S(1)}, f32[5,2048]{1,0:T(8,128)}, u32[]{:S(2)}) copy-start(f32[5,2048]{1,0:T(8,128)} %param.13) | copy-start | bytes 122884
  26.7 12.0 %copy-start.7 = (s32[16]{0:T(128)S(1)}, s32[16]{0:T(128)}, u32[]{:S(2)}) copy-start(s32[16]{0:T(128)} %param.14) | copy-start | bytes 196
  31.7 11.0 %collective-permute-start.3 = (bf16[32,4096]{1,0:T(8,128)(2,1)S(1)}, bf16[32,4096]{1,0:T(8,128)(2,1)S(1)}, u32[]{:S(2)}, u32[]{:S(2)}) collective-permute-start(bf16[32,4096]{1,0:T(8,128)(2,1)S(1)} %get-tuple-element.16), channel_id=1, source_target_pairs={{2,0},{4,2},{6,4},{8,6},{10,8},{12,10},{14,12},{3,1},{5,3},{7,5},{... | collective-permute-start | bytes 786440 | tf_op jit(solution)/shard_map/ppermute | solution.py:271
  33.0 21.1 %collective-permute-start.2 = (bf16[32,4096]{1,0:T(8,128)(2,1)S(1)}, bf16[32,4096]{1,0:T(8,128)(2,1)S(1)}, u32[]{:S(2)}, u32[]{:S(2)}) collective-permute-start(bf16[32,4096]{1,0:T(8,128)(2,1)S(1)} %get-tuple-element.17), channel_id=1, source_target_pairs={{0,2},{2,4},{4,6},{6,8},{8,10},{10,12},{12,14},{1,3},{3,5},{5,7},{... | collective-permute-start | bytes 786440 | tf_op jit(solution)/shard_map/ppermute | solution.py:270
  57.9 0.7 copy-start.1
  58.6 11.3 %collective-permute-start.6 = (bf16[128,4096]{1,0:T(8,128)(2,1)S(1)}, bf16[128,4096]{1,0:T(8,128)(2,1)S(1)}, u32[]{:S(2)}, u32[]{:S(2)}) collective-permute-start(bf16[128,4096]{1,0:T(8,128)(2,1)S(1)} %get-tuple-element.10), channel_id=1, source_target_pairs={{0,1},{1,0},{2,3},{3,2},{4,5},{5,4},{6,7},{7,6},{8,9},{9,8},{10,11... | collective-permute-start | bytes 3145736 | tf_op jit(solution)/shard_map/ppermute | solution.py:19
  69.6 8.7 %collective-permute-start.8 = (bf16[1024,1024]{1,0:T(8,128)(2,1)}, bf16[1024,1024]{1,0:T(8,128)(2,1)}, u32[]{:S(2)}, u32[]{:S(2)}) collective-permute-start(bf16[1024,1024]{1,0:T(8,128)(2,1)} %all-gather.3.cloned.1.call-done), channel_id=1, source_target_pairs={{0,1},{1,0},{2,3},{3,2},{4,5},{5,4},{6,7},{7,6},{8,9},{9,8},{10,11... | collective-permute-start | bytes 6291464 | tf_op jit(solution)/shard_map/ppermute | solution.py:19
  69.9 6.9 %copy-start.2 = (bf16[128,1024]{1,0:T(8,128)(2,1)S(1)}, bf16[128,1024]{1,0:T(8,128)(2,1)}, u32[]{:S(2)}) copy-start(bf16[128,1024]{1,0:T(8,128)(2,1)} %copy-done.1) | copy-start | bytes 786436
  76.2 1.7 %collective-permute-start.7 = (bf16[128,1024]{1,0:T(8,128)(2,1)S(1)}, bf16[128,1024]{1,0:T(8,128)(2,1)S(1)}, u32[]{:S(2)}, u32[]{:S(2)}) collective-permute-start(bf16[128,1024]{1,0:T(8,128)(2,1)S(1)} %convolution_convert_fusion.1), channel_id=1, source_target_pairs={{0,1},{1,0},{2,3},{3,2},{4,5},{5,4},{6,7},{7,6},{8,9},{9,8},{10,11... | collective-permute-start | bytes 786440 | tf_op jit(solution)/shard_map/ppermute | solution.py:19
  77.9 4.7 %slice-start = ((s8[8388608]{0:T(1024)(128)(4,1)}), s8[4194304]{0:T(1024)(128)(4,1)S(1)}, s32[]{:S(2)}) async-start(s8[8388608]{0:T(1024)(128)(4,1)} %bitcast.27), calls=%async_computation.2 | async-start | bytes 8388608
  78.3 4.3 %slice-start.1 = ((s8[8388608]{0:T(1024)(128)(4,1)}), s8[4194304]{0:T(1024)(128)(4,1)S(1)}, s32[]{:S(2)}) async-start(s8[8388608]{0:T(1024)(128)(4,1)} %bitcast.27), calls=%async_computation.3 | async-start | bytes 8388608
  78.4 4.6 %copy-start.8 = (bf16[1024,1024]{1,0:T(8,128)(2,1)S(1)}, bf16[1024,1024]{1,0:T(8,128)(2,1)}, u32[]{:S(2)}) copy-start(bf16[1024,1024]{1,0:T(8,128)(2,1)} %all-gather.3.cloned.1.call-done) | copy-start | bytes 6291460
  83.0 2.3 %copy-start.12 = (bf16[1024,1024]{1,0:T(8,128)(2,1)}, bf16[1024,1024]{1,0:T(8,128)(2,1)S(1)}, u32[]{:S(2)}) copy-start(bf16[1024,1024]{1,0:T(8,128)(2,1)S(1)} %fusion.19) | copy-start | bytes 6291460
  83.0 2.7 %copy-start.11 = (bf16[128,1024]{1,0:T(8,128)(2,1)S(1)}, bf16[128,1024]{1,0:T(8,128)(2,1)}, u32[]{:S(2)}) copy-start(bf16[128,1024]{1,0:T(8,128)(2,1)} %param.15) | copy-start | bytes 786436
  85.3 38.5 %collective-permute-start.9 = (bf16[1024,512]{1,0:T(8,128)(2,1)}, bf16[1024,512]{1,0:T(8,128)(2,1)S(1)}, u32[]{:S(2)}, u32[]{:S(2)}) collective-permute-start(bf16[1024,512]{1,0:T(8,128)(2,1)} %fusion.20), channel_id=1, source_target_pairs={{0,1},{1,0},{2,3},{3,2},{4,5},{5,4},{6,7},{7,6},{8,9},{9,8},{10,11... | collective-permute-start | bytes 3145736 | tf_op jit(solution)/shard_map/ppermute | solution.py:19
  129.2 3.3 %collective-permute-start.10 = (bf16[1024,512]{1,0:T(8,128)(2,1)S(1)}, bf16[1024,512]{1,0:T(8,128)(2,1)S(1)}, u32[]{:S(2)}, u32[]{:S(2)}) collective-permute-start(bf16[1024,512]{1,0:T(8,128)(2,1)S(1)} %shard_map.128), channel_id=1, source_target_pairs={{0,1},{1,0},{2,3},{3,2},{4,5},{5,4},{6,7},{7,6},{8,9},{9,8},{10,11... | collective-permute-start | bytes 3145736 | tf_op jit(solution)/shard_map/ppermute | solution.py:19
  132.5 3.1 %copy-start.9 = (bf16[1024,1024]{1,0:T(8,128)(2,1)S(1)}, bf16[1024,1024]{1,0:T(8,128)(2,1)}, u32[]{:S(2)}) copy-start(bf16[1024,1024]{1,0:T(8,128)(2,1)} %all-gather.3.cloned.1.call-done) | copy-start | bytes 6291460
Sparse Core Ops, SparseCore 0:
  10.7 58.8 all-gather.2
  71.8 50.6 all-gather.4

commit v2 on v1

--- a/solution.py
+++ b/solution.py
@@ -31,9 +31,45 @@
     return v.astype(BF16).astype(F32)
 
 
-def seq_kernel(fd_ref, md_ref, tied_ref, kf_ref, km_ref, cur_ref, prev_ref, next_ref, cot_ref,
-               cprev_ref, cnext_ref, hid_ref, out_ref, sg_ref, corr_ref, si, li, gs, gl):
+def seq_kernel(count, fd_ref, md_ref, tied_ref, kf_ref, km_ref, cur_ref, cot_ref, hid_ref, w_ref,
+               out_ref, corr_ref, near_ref, got_ref, col_ref, si, li, gs, gl, prev_ref, next_ref,
+               cprev_ref, cnext_ref, stack, wbuf, far, got, landed, wsem, hsend, hrecv, asend,
+               arecv, psend, precv):
     length, width = cot_ref.shape
+    cw = 4 * width // count
+    me = lax.axis_index("seq")
+    chan = lax.axis_index("chan")
+    part = lax.axis_index("groups")
+    load = pltpu.make_async_copy(w_ref, wbuf, wsem)
+    load.start()
+
+    def device(d, c):
+        return (part, lax.rem(me + d, count), lax.rem(chan + c, 2))
+
+    barrier = pltpu.get_barrier_semaphore()
+    for d in range(count):
+        pl.semaphore_signal(barrier, inc=1, device_id=device(d, 0 if d else 1), device_id_type=MESH)
+    pl.semaphore_wait(barrier, count)
+
+    def remote(src, dst, send, recv, to):
+        copy = pltpu.make_async_remote_copy(
+            src_ref=src, dst_ref=dst, send_sem=send, recv_sem=recv,
+            device_id=to, device_id_type=MESH,
+        )
+        copy.start()
+        return copy
+
+    tail, head = pl.ds(length - MARGIN, MARGIN), pl.ds(0, MARGIN)
+    halos = [
+        remote(cur_ref.at[tail], prev_ref, hsend.at[0], hrecv.at[0], device(1, 0)),
+        remote(cur_ref.at[head], next_ref, hsend.at[1], hrecv.at[1], device(count - 1, 0)),
+        remote(cot_ref.at[tail], cprev_ref, hsend.at[2], hrecv.at[2], device(1, 0)),
+        remote(cot_ref.at[head], cnext_ref, hsend.at[3], hrecv.at[3], device(count - 1, 0)),
+    ]
+    for copy in halos:
+        copy.wait()
+    has_prev = jnp.where(me > 0, 1.0, 0.0).astype(F32)
+    has_next = jnp.where(me < count - 1, 1.0, 0.0).astype(F32)
     corr_ref[...] = jnp.zeros_like(corr_ref)
 
     def group(g, carry):
@@ -43,7 +79,11 @@
         own = cols(0)
 
         def rows3(a, b, c, s):
-            return (a[:, cols(s)].astype(F32), b[:, cols(s)].astype(F32), c[:, cols(s)].astype(F32))
+            return (
+                a[:, cols(s)].astype(F32) * has_prev,
+                b[:, cols(s)].astype(F32),
+                c[:, cols(s)].astype(F32) * has_next,
+            )
 
         def fill(buf, parts):
             buf[0:MARGIN, :] = parts[0]
@@ -88,65 +128,40 @@
         out_ref[:, own] = (
             hid_ref[:, own].astype(F32) + sgate[1] * short_out + lgate[1] * long_out
         ).astype(BF16)
-        sg_ref[:, cols(0)] = d_short.astype(BF16)
-        sg_ref[:, cols(1)] = (bwd + rounded(mirb)).astype(BF16)
-        sg_ref[:, cols(2)] = (cot * short_out).astype(BF16)
-        sg_ref[:, cols(3)] = (cot * long_out).astype(BF16)
+        stack[chan, :, cols(0)] = d_short.astype(BF16)
+        stack[chan, :, cols(1)] = (bwd + rounded(mirb)).astype(BF16)
+        stack[chan, :, cols(2)] = (cot * short_out).astype(BF16)
+        stack[chan, :, cols(3)] = (cot * long_out).astype(BF16)
         return carry
 
     lax.fori_loop(0, width // GW, group, 0)
-
-
-def col_kernel(meta_ref, fd_ref, md_ref, tied_ref, kf_ref, km_ref, x_ref, cot_ref, sg_ref, buf):
-    length, width = cot_ref.shape
-    stream = meta_ref[0]
-    step = 128
-    buf[0:MARGIN, :] = jnp.zeros((MARGIN, GW), F32)
-    buf[MARGIN + length:, :] = jnp.zeros((MARGIN, GW), F32)
-
-    def run(back, short, g):
-        own = pl.ds(pl.multiple_of(g * GW, GW), GW)
-        sign = -1 if back else 1
-
-        def load(i, carry):
-            at = pl.multiple_of(i * step, step)
-            v = x_ref[pl.ds(at, step), own].astype(F32)
-            if back:
-                v = v * cot_ref[pl.ds(at, step), own].astype(F32)
-                if not short:
-                    v = rounded(v)
-            buf[pl.ds(at + MARGIN, step), :] = v
-            return carry
-
-        lax.fori_loop(0, length // step, load, 0)
-        fd, md = fd_ref[g], md_ref[g]
-
-        def body(i, carry):
-            at = pl.multiple_of(i * step, step)
-            base = at + MARGIN
-            acc = jnp.zeros((step, GW), F32)
-            if short:
-                for t in range(7):
-                    acc += tied_ref[t:t + 1, own] * buf[pl.ds(base + sign * (t - 3), step), :]
-            else:
-                mir = jnp.zeros((step, GW), F32)
-                for t in range(5):
-                    acc += kf_ref[t:t + 1, own] * buf[pl.ds(base + sign * (t - 2) * fd, step), :]
-                    mir += km_ref[t:t + 1, own] * buf[pl.ds(base - sign * (t - 2) * md, step), :]
-                acc += rounded(mir)
-            if not back:
-                acc = acc * cot_ref[pl.ds(at, step), own].astype(F32)
-            sg_ref[pl.ds(at, step), own] = acc.astype(BF16)
-            return carry
-
-        lax.fori_loop(0, length // step, body, 0)
-
-    def group(g, carry):
-        for s in range(4):
-            pl.when(stream == s)(functools.partial(run, s < 2, s % 2 == 0, g))
+    swapped = remote(stack.at[chan], stack.at[chan], psend.at[0], precv.at[0], device(0, 1))
+    sends = []
+    for d in range(1, count):
+        at = pl.multiple_of(lax.rem(me + d, count) * cw, GW)
+        sends.append(
+            remote(stack.at[chan, :, pl.ds(at, cw)], landed.at[me], asend.at[d], arecv.at[d],
+                   device(d, 0))
+        )
+    landed[me] = stack[chan, :, pl.ds(pl.multiple_of(me * cw, GW), cw)]
+    load.wait()
+    swapped.wait()
+    step = 2 * GW
+
+    def back(i, carry):
+        at = pl.ds(pl.multiple_of(i * step, step), step)
+        term = mm_t(stack[...].reshape(2 * length, 4 * width), wbuf[at, :])
+        near_ref[:, at] = term[:length]
+        far[:, at] = term[length:].astype(BF16)
         return carry
 
-    lax.fori_loop(0, width // GW, group, 0)
+    lax.fori_loop(0, width // step, back, 0)
+    crossed = remote(far, got, psend.at[1], precv.at[1], device(0, 1))
+    crossed.wait()
+    got_ref[...] = got[...]
+    for copy in sends:
+        copy.wait()
+    col_ref[...] = landed[...]
 
 
 def sum_kernel(count, x_ref, o_ref, got, mine, full, ssem, rsem, bssem, brsem):
@@ -257,7 +272,6 @@
 
     cot = mm(cotangent, order).astype(BF16)
     all_hidden = lax.all_gather(hidden, "seq", axis=0, tiled=True)
-    all_cot = lax.all_gather(cot, "seq", axis=0, tiled=True)
 
     turned = mm(swap(hidden), turn).astype(BF16)
     hid = mm(hidden, order).astype(BF16)
@@ -265,33 +279,45 @@
     near = mm(jnp.where(low, hidden, turned), weight)
     streams = (near + swap(far).astype(F32)).astype(BF16)
 
-    up = [(i, i + 1) for i in range(count - 1)]
-    down = [(i + 1, i) for i in range(count - 1)]
-    prev = lax.ppermute(streams[length - MARGIN:], "seq", up)
-    nxt = lax.ppermute(streams[:MARGIN], "seq", down)
-    cprev = lax.ppermute(cot[length - MARGIN:], "seq", up)
-    cnext = lax.ppermute(cot[:MARGIN], "seq", down)
+    cw = weight.shape[1] // count
     span = length + 2 * MARGIN
-    block, sg, corr = pl.pallas_call(
-        seq_kernel,
+    block, corr, near, far, col_sg = pl.pallas_call(
+        functools.partial(seq_kernel, count),
         out_shape=(
             jax.ShapeDtypeStruct((length, width), BF16),
-            jax.ShapeDtypeStruct((length, 4 * width), BF16),
             jax.ShapeDtypeStruct((17, width), F32),
+            jax.ShapeDtypeStruct((length, width), F32),
+            jax.ShapeDtypeStruct((length, width), BF16),
+            jax.ShapeDtypeStruct((count, length, cw), BF16),
         ),
-        in_specs=[smem()] * 2 + [vmem()] * 10,
-        out_specs=(vmem(),) * 3,
-        scratch_shapes=[pltpu.VMEM((span, GW), F32)] * 4,
-        compiler_params=pltpu.CompilerParams(vmem_limit_bytes=32 * 2**20),
-        cost_estimate=pl.CostEstimate(flops=10**7, bytes_accessed=2 * 10**7, transcendentals=0),
-    )(fd, md, tied, kf, km, streams, prev, nxt, cot, cprev, cnext, hid)
+        in_specs=[smem()] * 2 + [vmem()] * 6 + [pl.BlockSpec(memory_space=pl.ANY)],
+        out_specs=(vmem(),) * 5,
+        scratch_shapes=[pltpu.VMEM((span, GW), F32)] * 4
+        + [pltpu.VMEM((MARGIN, 4 * width), BF16)] * 2
+        + [pltpu.VMEM((MARGIN, width), BF16)] * 2
+        + [
+            pltpu.VMEM((2, length, 4 * width), BF16),
+            pltpu.VMEM((width, 4 * width), BF16),
+            pltpu.VMEM((length, width), BF16),
+            pltpu.VMEM((length, width), BF16),
+            pltpu.VMEM((count, length, cw), BF16),
+            pltpu.SemaphoreType.DMA,
+            pltpu.SemaphoreType.DMA((4,)),
+            pltpu.SemaphoreType.DMA((4,)),
+            pltpu.SemaphoreType.DMA((count,)),
+            pltpu.SemaphoreType.DMA((count,)),
+            pltpu.SemaphoreType.DMA((2,)),
+            pltpu.SemaphoreType.DMA((2,)),
+        ],
+        compiler_params=pltpu.CompilerParams(
+            vmem_limit_bytes=40 * 2**20, collective_id=1, has_side_effects=True
+        ),
+        cost_estimate=pl.CostEstimate(
+            flops=3 * 10**9, bytes_accessed=5 * 10**7, transcendentals=0
+        ),
+    )(fd, md, tied, kf, km, streams, cot, hid, weight)
     block_result_output = mm(block, order).astype(BF16)
-
-    other_sg = swap(sg)
-    sg0, sg1 = jnp.where(low, sg, other_sg), jnp.where(low, other_sg, sg)
-    far = mm_t(sg1, weight).astype(BF16)
-    near = mm_t(sg0, weight)
-    hidden_input_gradient = cotangent.astype(F32) + near + mm(swap(far), turn)
+    hidden_input_gradient = cotangent.astype(F32) + near + mm(far, turn)
 
     embedding = jnp.stack(
         [
@@ -302,38 +328,8 @@
     small = jnp.concatenate([corr, embedding, jnp.zeros((3, width), F32)], axis=0)
     summed = all_sum(small, count)
 
-    cw = weight.shape[1] // count
-    per = count // 4
-    stream = me // per
-    first = lax.rem(me, per) * cw
-    source = lax.rem(me + count // 2, count) * cw
     all_turned = mm(swap(all_hidden), turn).astype(BF16)
-    columns = lax.dynamic_slice_in_dim(weight, source, cw, 1)
-    far = mm(jnp.where(low, all_turned, all_hidden), columns).astype(BF16)
-    near = mm(jnp.where(low, all_hidden, all_turned), columns)
-    values = (near + swap(far).astype(F32)).astype(BF16)
-
-    def here(v):
-        return lax.dynamic_slice_in_dim(v, first, cw, 1)
-
-    col_sg = pl.pallas_call(
-        col_kernel,
-        out_shape=jax.ShapeDtypeStruct(values.shape, BF16),
-        in_specs=[smem()] * 3 + [vmem()] * 5,
-        out_specs=vmem(),
-        scratch_shapes=[pltpu.VMEM((values.shape[0] + 2 * MARGIN, GW), F32)],
-        compiler_params=pltpu.CompilerParams(vmem_limit_bytes=32 * 2**20),
-        cost_estimate=pl.CostEstimate(flops=10**7, bytes_accessed=10**7, transcendentals=0),
-    )(
-        stream.reshape(1),
-        lax.dynamic_slice_in_dim(fd, first // GW, cw // GW, 0),
-        lax.dynamic_slice_in_dim(md, first // GW, cw // GW, 0),
-        here(tied),
-        here(kf),
-        here(km),
-        values,
-        here(all_cot),
-    )
+    col_sg = col_sg.reshape(count * length, cw)
     other = swap(col_sg)
     rows = (((0,), (0,)), ((), ()))
     mixing_half_gradient = lax.dot_general(

time: 146 us -> 130 us (0.89)
  Pallas kernels: 21.1 us -> 76.4 us
  waiting for transfers between devices: 43.2 us -> 0.05 us
  matrix products: 38 us -> 23.6 us
  starting transfers between devices: 15.5 us -> 1.4 us
  other arithmetic: 4.52 us -> 6.27 us
    pallas_call x2 -> x1, Pallas kernels: 6.15 us -> 55.2 us  [local(): pl.pallas_call(functools.partial(seq_kernel, count), out_shape=(jax.Shape...]
    all_gather x1 -> x0, waiting for transfers between devices: 15.9 us -> none  [local(): all_cot = lax.all_gather(cot, 'seq', axis=0, tiled=True)]
    ppermute x4 -> x0, waiting for transfers between devices: 15.2 us -> none  [the longest x1 11.4 us: local(): prev = lax.ppermute(streams[length - MARGIN:], 'seq', up)]
    ppermute x4 -> x0, starting transfers between devices: 13.4 us -> none  [the longest x1 5.62 us: local(): prev = lax.ppermute(streams[length - MARGIN:], 'seq', up)]
    all_gather x1, waiting for transfers between devices: 11.1 us -> 0.02 us  [local(): all_hidden = lax.all_gather(hidden, 'seq', axis=0, tiled=True)]
    dot_general x2 -> x0, matrix products: 10.2 us -> none  [mm_t(): lax.dot_general(a, b, (((1,), (1,)), ((), ())), preferred_element_type=F32)]
    dot_general x10 -> x7, matrix products: 22.2 us -> 12.7 us  [mm(): return jnp.dot(a, b, preferred_element_type=F32)]
    pallas_call x1, Pallas kernels: 15 us -> 21.2 us  [all_sum(): pl.pallas_call(functools.partial(sum_kernel, count), out_shape=jax.ShapeD...]
  transfers between devices with their start and end apart: 13 -> 5, of which waited for: 5 -> 0; matrix products, arithmetic and copies ran while one was open for 26% -> 17% of each run, Pallas kernels for 13% -> 59%
where the time goes in v2:
time: 130 us; the launch traced here: 129 us
  Pallas kernels  76.4 us (59%)
  matrix products  23.6 us (18%)
  between operations  14.3 us (11%)
  local copies, waits for them, and re-layouts  7.38 us (6%)
  other arithmetic  6.27 us (5%)
  starting transfers between devices  1.4 us (1%)
    pallas_call x1, Pallas kernels, local(): pl.pallas_call(functools.partial(seq_kernel, count), out_shape=(jax.Shape...  55.2 us
    pallas_call x1, Pallas kernels, all_sum(): pl.pallas_call(functools.partial(sum_kernel, count), out_shape=jax.ShapeD...  21.2 us
    dot_general x7, matrix products, mm(): return jnp.dot(a, b, preferred_element_type=F32)  12.7 us
    dot_general x1, matrix products, local(): lax.dot_general(all_turned, jnp.where(low, other, col_sg), rows, preferre...  6.71 us
    dot_general x1, matrix products, local(): lax.dot_general(all_hidden, jnp.where(low, col_sg, other), rows, preferre...  4.2 us
  transfers between devices with their start and end apart: 5, of which 0 were waited for; matrix products, arithmetic and copies ran while one was open for 17% of the time, Pallas kernels for 59%

profile of v2, /device:TPU:0, one launch (start us, length us, event | category | flops | bytes accessed | tf_op | source)
XLA Modules:
  0.0 129.3 jit_solution(8263738091880615307)
XLA Ops:
  7.2 0.7 dynamic-slice_convert_fusion
  7.9 0.7 broadcast_compare_fusion.3
  8.6 1.9 %add_convert_fusion.1 = bf16[128,1024]{1,0:T(8,128)(2,1)} fusion(bf16[128,1024]{1,0:T(8,128)(2,1)} %param.8, f32[1024]{0:T(1024)S(1)} %bitcast.34, f32[1024]{0:T(1024)S(1)} %bitcast.35, f32[1024]{0:T(1024)S(1)} %bitcast.36, f32[1024]{0:T(1024)S(1)} %bitcast.33, pred[128]{0:T(512)(128)(4,1)S(1)} %get-tuple-element.37, ...), kind=kLoop, calls=%fused_computation.31 | loop fusion | flops 1310720 | bytes 541184 | tf_op jit(solution)/shard_map/convert_element_type | solution.py:258
  10.5 0.5 collective-permute-start
  11.1 0.7 slice.72
  11.9 0.8 fusion.47
  12.7 0.4 fusion.24
  13.2 4.7 %convolution_convert_fusion = bf16[128,4096]{1,0:T(8,128)(2,1)S(1)} fusion(bf16[1024,4096]{1,0:T(8,128)(2,1)} %w_ref.1, bf16[128,1024]{1,0:T(8,128)(2,1)S(1)} %fusion.24, bf16[128,1024]{1,0:T(8,128)(2,1)} %add_convert_fusion.1, pred[]{:T(512)S(6)} %eq.44), kind=kOutput, calls=%fused_computation | convolution fusion | flops 1074397184 | bytes 9961473 | tf_op jit(solution)/shard_map/dot_general | solution.py:23
  17.9 0.3 collective-permute-start.1
  18.2 0.6 slice.76
  18.8 0.6 rev.18
  19.6 0.6 slice.79
  20.2 0.5 fusion.25.cot_ref
  20.7 0.4 fusion.18.hid_ref
  21.2 5.0 %add_convert_fusion.cur_ref = bf16[128,4096]{1,0:T(8,128)(2,1)S(1)} fusion(bf16[128,4096]{1,0:T(8,128)(2,1)S(1)} %collective-permute-done.1, bf16[1024,4096]{1,0:T(8,128)(2,1)} %w_ref.1, bf16[128,1024]{1,0:T(8,128)(2,1)S(1)} %copy-done, bf16[128,1024]{1,0:T(8,128)(2,1)S(1)} %fusion.24, pred[]{:T(512)S(6)} %eq.44), kind=kOutput, calls=%fused_computation.9 | convolution fusion | flops 1075445760 | bytes 11010049 | tf_op jit(solution)/shard_map/dot_general | solution.py:23
  26.2 0.6 slice-done.1
  26.8 55.2 %shard_map.127 = (bf16[128,1024]{1,0:T(8,128)(2,1)S(1)}, f32[17,1024]{1,0:T(8,128)S(1)}, f32[128,1024]{1,0:T(8,128)S(1)}, bf16[128,1024]{1,0:T(8,128)(2,1)S(1)}, bf16[8,128,512]{2,1,0:T(8,128)(2,1)S(1)}) custom-call(s32[8]{0:T(128)S(1)} %get-tuple-element.34.fd_ref, s32[8]{0:T(128)S(1)} %get-tuple-element.33.md_ref, f32[7,1024]{1,0:T(8,128)S(1)} %add_select_fusion.tied_ref, ...), custom_call_target="tpu_custom_call" | custom-call | flops 3000000000 | bytes 50000000 | tf_op jit(solution)/shard_map/pallas_call | solution.py:284
  82.1 0.5 collective-permute-start.3
  82.6 0.4 fusion.1
  83.0 1.0 select_reduce_fusion
  84.1 0.7 reshape.32.x_ref
  84.8 21.2 %shard_map.128 = f32[2,8,24,128]{3,2,1,0:T(8,128)} custom-call(f32[8,24,128]{2,1,0:T(8,128)} %reshape.32.x_ref), custom_call_target="tpu_custom_call" | custom-call | flops 1000000 | bytes 1000000 | tf_op jit(solution)/shard_map/pallas_call | solution.py:229
  106.0 1.0 fusion.46
  107.0 0.2 rev.20
  107.3 0.7 rev.21
  107.9 0.6 rev.22
  108.5 0.6 pad_maximum_fusion.2
  109.1 0.6 pad_maximum_fusion
  109.8 0.6 pad_maximum_fusion.1
  110.4 1.1 fusion.21
  111.6 6.7 %fusion.4 = f32[1024,512]{1,0:T(8,128)} fusion(bf16[1024,1024]{1,0:T(8,128)(2,1)} %collective-permute-done.3, bf16[1024,512]{1,0:T(8,128)(2,1)} %collective-permute-done.2, bf16[1024,512]{1,0:T(8,128)(2,1)S(1)} %bitcast.27, pred[]{:T(512)S(6)} %eq.44), kind=kOutput, calls=%fused_computation.7 | convolution fusion | flops 3224895488 | bytes 6291457 | tf_op jit(solution)/shard_map/dot_general | solution.py:337
  118.3 4.2 %convolution_add_fusion = f32[1024,512]{1,0:T(8,128)} fusion(f32[1024,512]{1,0:T(8,128)} %fusion.4, bf16[1024,1024]{1,0:T(8,128)(2,1)S(1)} %copy-done.5, bf16[1024,512]{1,0:T(8,128)(2,1)S(1)} %bitcast.28, bf16[1024,512]{1,0:T(8,128)(2,1)} %collective-permute-done.2, pred[]{:T(512)S(6)} %eq.44), kind=kOutput, calls=%fused_computation.16 | convolution fusion | flops 1074790400 | bytes 8388609 | tf_op jit(solution)/shard_map/dot_general | solution.py:335
  (41 shorter events, 0.7 us)
Async XLA Ops:
  7.2 74.9 %all-gather.2.cloned.1.call-start = ((), (), s32[]{:S(2)}) async-start(), calls=%async_computation | async-start | bytes 2359296 | tf_op jit(solution)/shard_map/all_gather | solution.py:274
  10.5 2.1 %collective-permute-start = (bf16[128,1024]{1,0:T(8,128)(2,1)}, bf16[128,1024]{1,0:T(8,128)(2,1)S(1)}, u32[]{:S(2)}, u32[]{:S(2)}) collective-permute-start(bf16[128,1024]{1,0:T(8,128)(2,1)} %add_convert_fusion.1), channel_id=1, source_target_pairs={{0,1},{1,0},{2,3},{3,2},{4,5},{5,4},{6,7},{7,6},{8,9},{9,8},{10,11... | collective-permute-start | bytes 786440 | tf_op jit(solution)/shard_map/ppermute | solution.py:19
  13.1 5.1 %copy-start.4 = (s32[16]{0:T(128)S(1)}, s32[16]{0:T(128)}, u32[]{:S(2)}) copy-start(s32[16]{0:T(128)} %param.14) | copy-start | bytes 196
  13.1 6.5 %slice-start.2 = ((f32[5,2048]{1,0:T(8,128)}), f32[5,1024]{1,0:T(8,128)S(1)}, s32[]{:S(2)}) async-start(f32[5,2048]{1,0:T(8,128)} %param.13), calls=%async_computation.3 | async-start | bytes 65536 | tf_op jit(solution)/shard_map/slice | solution.py:268
  13.1 7.1 %copy-start.3 = (f32[5,2048]{1,0:T(8,128)S(1)}, f32[5,2048]{1,0:T(8,128)}, u32[]{:S(2)}) copy-start(f32[5,2048]{1,0:T(8,128)} %param.13) | copy-start | bytes 122884
  13.1 7.1 %copy-start.2 = (f32[7,2048]{1,0:T(8,128)S(1)}, f32[7,2048]{1,0:T(8,128)}, u32[]{:S(2)}) copy-start(f32[7,2048]{1,0:T(8,128)} %param.12) | copy-start | bytes 172036
  13.1 7.1 %copy-start.1 = (bf16[128,1024]{1,0:T(8,128)(2,1)S(1)}, bf16[128,1024]{1,0:T(8,128)(2,1)}, u32[]{:S(2)}) copy-start(bf16[128,1024]{1,0:T(8,128)(2,1)} %param.15) | copy-start | bytes 786436
  17.9 2.8 %copy-start = (bf16[128,1024]{1,0:T(8,128)(2,1)S(1)}, bf16[128,1024]{1,0:T(8,128)(2,1)}, u32[]{:S(2)}) copy-start(bf16[128,1024]{1,0:T(8,128)(2,1)} %add_convert_fusion.1) | copy-start | bytes 786436
  17.9 3.3 %collective-permute-start.1 = (bf16[128,4096]{1,0:T(8,128)(2,1)S(1)}, bf16[128,4096]{1,0:T(8,128)(2,1)S(1)}, u32[]{:S(2)}, u32[]{:S(2)}) collective-permute-start(bf16[128,4096]{1,0:T(8,128)(2,1)S(1)} %convolution_convert_fusion), channel_id=1, source_target_pairs={{0,1},{1,0},{2,3},{3,2},{4,5},{5,4},{6,7},{7,6},{8,9},{9,8},{10,11... | collective-permute-start | bytes 3145736 | tf_op jit(solution)/shard_map/ppermute | solution.py:19
  20.7 5.5 %slice-start = ((s8[8388608]{0:T(1024)(128)(4,1)}), s8[4194304]{0:T(1024)(128)(4,1)S(1)}, s32[]{:S(2)}) async-start(s8[8388608]{0:T(1024)(128)(4,1)} %bitcast.24), calls=%async_computation.1 | async-start | bytes 8388608
  21.2 5.6 %slice-start.1 = ((s8[8388608]{0:T(1024)(128)(4,1)}), s8[4194304]{0:T(1024)(128)(4,1)S(1)}, s32[]{:S(2)}) async-start(s8[8388608]{0:T(1024)(128)(4,1)} %bitcast.24), calls=%async_computation.2 | async-start | bytes 8388608
  82.0 29.6 %collective-permute-start.2 = (bf16[1024,512]{1,0:T(8,128)(2,1)S(1)}, bf16[1024,512]{1,0:T(8,128)(2,1)}, u32[]{:S(2)}, u32[]{:S(2)}) collective-permute-start(bf16[1024,512]{1,0:T(8,128)(2,1)S(1)} %bitcast.26), channel_id=1, source_target_pairs={{0,1},{1,0},{2,3},{3,2},{4,5},{5,4},{6,7},{7,6},{8,9},{9,8},{10,11... | collective-permute-start | bytes 3145736 | tf_op jit(solution)/shard_map/ppermute | solution.py:19
  82.1 29.5 %collective-permute-start.3 = (bf16[1024,1024]{1,0:T(8,128)(2,1)}, bf16[1024,1024]{1,0:T(8,128)(2,1)}, u32[]{:S(2)}, u32[]{:S(2)}) collective-permute-start(bf16[1024,1024]{1,0:T(8,128)(2,1)} %all-gather.2.cloned.1.call-done), channel_id=1, source_target_pairs={{0,1},{1,0},{2,3},{3,2},{4,5},{5,4},{6,7},{7,6},{8,9},{9,8},{10,11... | collective-permute-start | bytes 6291464 | tf_op jit(solution)/shard_map/ppermute | solution.py:19
  111.6 6.7 %copy-start.5 = (bf16[1024,1024]{1,0:T(8,128)(2,1)S(1)}, bf16[1024,1024]{1,0:T(8,128)(2,1)}, u32[]{:S(2)}) copy-start(bf16[1024,1024]{1,0:T(8,128)(2,1)} %all-gather.2.cloned.1.call-done) | copy-start | bytes 6291460
Sparse Core Ops, SparseCore 0:
  10.7 69.2 all-gather.1

commit v3 on v2

--- a/solution.py
+++ b/solution.py
@@ -31,10 +31,10 @@
     return v.astype(BF16).astype(F32)
 
 
-def seq_kernel(count, fd_ref, md_ref, tied_ref, kf_ref, km_ref, cur_ref, cot_ref, hid_ref, w_ref,
-               out_ref, corr_ref, near_ref, got_ref, col_ref, si, li, gs, gl, prev_ref, next_ref,
+def seq_kernel(count, fd_ref, md_ref, tied_ref, kf_ref, km_ref, cur_ref, cot_ref, hid_ref, cotn_ref, hot_ref, w_ref,
+               out_ref, sum_ref, near_ref, got_ref, col_ref, si, li, gs, gl, prev_ref, next_ref,
                cprev_ref, cnext_ref, stack, wbuf, far, got, landed, wsem, hsend, hrecv, asend,
-               arecv, psend, precv):
+               arecv, psend, precv, small, parts, mine, full, ssend, srecv, bsend, brecv):
     length, width = cot_ref.shape
     cw = 4 * width // count
     me = lax.axis_index("seq")
@@ -47,9 +47,10 @@
         return (part, lax.rem(me + d, count), lax.rem(chan + c, 2))
 
     barrier = pltpu.get_barrier_semaphore()
-    for d in range(count):
-        pl.semaphore_signal(barrier, inc=1, device_id=device(d, 0 if d else 1), device_id_type=MESH)
-    pl.semaphore_wait(barrier, count)
+    peers = [(d, c) for d in range(count) for c in range(2) if d or c]
+    for d, c in peers:
+        pl.semaphore_signal(barrier, inc=1, device_id=device(d, c), device_id_type=MESH)
+    pl.semaphore_wait(barrier, len(peers))
 
     def remote(src, dst, send, recv, to):
         copy = pltpu.make_async_remote_copy(
@@ -70,7 +71,7 @@
         copy.wait()
     has_prev = jnp.where(me > 0, 1.0, 0.0).astype(F32)
     has_next = jnp.where(me < count - 1, 1.0, 0.0).astype(F32)
-    corr_ref[...] = jnp.zeros_like(corr_ref)
+    small[...] = jnp.zeros_like(small)
 
     def group(g, carry):
         def cols(s):
@@ -107,7 +108,7 @@
             tap = tied_ref[t:t + 1, own]
             view = si[MARGIN + t - 3:MARGIN + t - 3 + length, :]
             short_out += tap * view
-            corr_ref[t:t + 1, own] = jnp.sum(sgrad[1] * view, axis=0, keepdims=True)
+            small[t, pl.ds(g, 1), :] = jnp.sum(sgrad[1] * view, axis=0, keepdims=True)
             d_short += tap * gs[MARGIN - t + 3:MARGIN - t + 3 + length, :]
         fwd = jnp.zeros((length, GW), F32)
         bwd = jnp.zeros((length, GW), F32)
@@ -118,10 +119,10 @@
             km = km_ref[t:t + 1, own]
             view = li[pl.ds(MARGIN + (t - 2) * fd, length), :]
             fwd += kf * view
-            corr_ref[7 + t:8 + t, own] = jnp.sum(lgrad[1] * view, axis=0, keepdims=True)
+            small[7 + t, pl.ds(g, 1), :] = jnp.sum(lgrad[1] * view, axis=0, keepdims=True)
             view = li[pl.ds(MARGIN - (t - 2) * md, length), :]
             mir += km * view
-            corr_ref[12 + t:13 + t, own] = jnp.sum(lgrad[1] * view, axis=0, keepdims=True)
+            small[12 + t, pl.ds(g, 1), :] = jnp.sum(lgrad[1] * view, axis=0, keepdims=True)
             bwd += kf * gl[pl.ds(MARGIN - (t - 2) * fd, length), :]
             mirb += km * gl[pl.ds(MARGIN + (t - 2) * md, length), :]
         long_out = fwd + rounded(mir)
@@ -159,91 +160,53 @@
     crossed = remote(far, got, psend.at[1], precv.at[1], device(0, 1))
     crossed.wait()
     got_ref[...] = got[...]
+
+    hot = hot_ref[...]
+    rest = cotn_ref[...].astype(F32) + near_ref[...]
+    table = jnp.zeros((hot.shape[0], width), F32)
+    for _ in range(3):
+        piece = rest.astype(BF16)
+        table += mm(hot, piece)
+        rest = rest - piece.astype(F32)
+    turned = mm(hot, got[...])
+    for i in range(width // GW):
+        for b in range(4):
+            at = slice(i * GW, (i + 1) * GW)
+            small[17 + b, i:i + 1, :] = table[b:b + 1, at]
+            small[21 + b, i:i + 1, :] = turned[b:b + 1, at]
+
+    share = small.shape[0] // count
+    shares = []
+    for d in range(1, count):
+        at = pl.ds(lax.rem(me + d, count) * share, share)
+        shares.append(remote(small.at[at], parts.at[d], ssend.at[d], srecv.at[d], device(d, 0)))
+    own_rows = pl.ds(me * share, share)
+    total = small[own_rows]
+    for d in range(1, count):
+        shares[d - 1].wait_recv()
+        total = total + parts[d]
+    mine[...] = total
+    casts = [
+        remote(mine, full.at[chan, own_rows], bsend.at[d, c], brecv.at[d, c], device(d, c))
+        for d, c in peers
+    ]
+    full[chan, own_rows] = total
+    for copy in casts:
+        copy.wait()
+    for copy in shares:
+        copy.wait_send()
+    sum_ref[...] = full[...]
     for copy in sends:
         copy.wait()
     col_ref[...] = landed[...]
 
 
-def sum_kernel(count, x_ref, o_ref, got, mine, full, ssem, rsem, bssem, brsem):
-    me = lax.axis_index("seq")
-    chan = lax.axis_index("chan")
-    part = lax.axis_index("groups")
-    peers = [(d, c) for d in range(count) for c in range(2) if d or c]
-
-    def device(d, c):
-        return (part, lax.rem(me + d, count), lax.rem(chan + c, 2))
-
-    barrier = pltpu.get_barrier_semaphore()
-    for d, c in peers:
-        pl.semaphore_signal(barrier, inc=1, device_id=device(d, c), device_id_type=MESH)
-    pl.semaphore_wait(barrier, len(peers))
-    sends = []
-    for d in range(1, count):
-        copy = pltpu.make_async_remote_copy(
-            src_ref=x_ref.at[lax.rem(me + d, count)],
-            dst_ref=got.at[d],
-            send_sem=ssem.at[d],
-            recv_sem=rsem.at[d],
-            device_id=device(d, 0),
-            device_id_type=MESH,
-        )
-        copy.start()
-        sends.append(copy)
-    total = x_ref[me]
-    for d in range(1, count):
-        sends[d - 1].wait_recv()
-        total = total + got[d]
-    mine[...] = total
-    casts = []
-    for d, c in peers:
-        copy = pltpu.make_async_remote_copy(
-            src_ref=mine,
-            dst_ref=full.at[chan, me],
-            send_sem=bssem.at[d, c],
-            recv_sem=brsem.at[d, c],
-            device_id=device(d, c),
-            device_id_type=MESH,
-        )
-        copy.start()
-        casts.append(copy)
-    full[chan, me] = total
-    for copy in casts:
-        copy.wait_recv()
-    o_ref[...] = full[...]
-    for copy in sends + casts:
-        copy.wait_send()
-
-
 def vmem():
     return pl.BlockSpec(memory_space=pltpu.VMEM)
 
 
 def smem():
     return pl.BlockSpec(memory_space=pltpu.SMEM)
-
-
-def all_sum(values, count):
-    rows, width = values.shape
-    lines = rows * width // (count * 128)
-    x = values.reshape(count, lines, 128)
-    out = pl.pallas_call(
-        functools.partial(sum_kernel, count),
-        out_shape=jax.ShapeDtypeStruct((2, count, lines, 128), F32),
-        in_specs=[vmem()],
-        out_specs=vmem(),
-        scratch_shapes=[
-            pltpu.VMEM((count, lines, 128), F32),
-            pltpu.VMEM((lines, 128), F32),
-            pltpu.VMEM((2, count, lines, 128), F32),
-            pltpu.SemaphoreType.DMA((count,)),
-            pltpu.SemaphoreType.DMA((count,)),
-            pltpu.SemaphoreType.DMA((count, 2)),
-            pltpu.SemaphoreType.DMA((count, 2)),
-        ],
-        compiler_params=pltpu.CompilerParams(collective_id=0, has_side_effects=True),
-        cost_estimate=pl.CostEstimate(flops=10**6, bytes_accessed=10**6, transcendentals=0),
-    )(x)
-    return out.reshape(2, rows, width)
 
 
 def local(residual, index, table, weight, short_taps, long_taps, dilations, cotangent):
@@ -279,18 +242,19 @@
     near = mm(jnp.where(low, hidden, turned), weight)
     streams = (near + swap(far).astype(F32)).astype(BF16)
 
+    hot = (jnp.arange(16, dtype=jnp.int32)[:, None] == index[None, :]).astype(BF16)
     cw = weight.shape[1] // count
     span = length + 2 * MARGIN
-    block, corr, near, far, col_sg = pl.pallas_call(
+    block, summed, near, far, col_sg = pl.pallas_call(
         functools.partial(seq_kernel, count),
         out_shape=(
             jax.ShapeDtypeStruct((length, width), BF16),
-            jax.ShapeDtypeStruct((17, width), F32),
+            jax.ShapeDtypeStruct((2, 32, groups, GW), F32),
             jax.ShapeDtypeStruct((length, width), F32),
             jax.ShapeDtypeStruct((length, width), BF16),
             jax.ShapeDtypeStruct((count, length, cw), BF16),
         ),
-        in_specs=[smem()] * 2 + [vmem()] * 6 + [pl.BlockSpec(memory_space=pl.ANY)],
+        in_specs=[smem()] * 2 + [vmem()] * 8 + [pl.BlockSpec(memory_space=pl.ANY)],
         out_specs=(vmem(),) * 5,
         scratch_shapes=[pltpu.VMEM((span, GW), F32)] * 4
         + [pltpu.VMEM((MARGIN, 4 * width), BF16)] * 2
@@ -308,6 +272,14 @@
             pltpu.SemaphoreType.DMA((count,)),
             pltpu.SemaphoreType.DMA((2,)),
             pltpu.SemaphoreType.DMA((2,)),
+            pltpu.VMEM((32, groups, GW), F32),
+            pltpu.VMEM((count, 32 // count, groups, GW), F32),
+            pltpu.VMEM((32 // count, groups, GW), F32),
+            pltpu.VMEM((2, 32, groups, GW), F32),
+            pltpu.SemaphoreType.DMA((count,)),
+            pltpu.SemaphoreType.DMA((count,)),
+            pltpu.SemaphoreType.DMA((count, 2)),
+            pltpu.SemaphoreType.DMA((count, 2)),
         ],
         compiler_params=pltpu.CompilerParams(
             vmem_limit_bytes=40 * 2**20, collective_id=1, has_side_effects=True
@@ -315,19 +287,11 @@
         cost_estimate=pl.CostEstimate(
             flops=3 * 10**9, bytes_accessed=5 * 10**7, transcendentals=0
         ),
-    )(fd, md, tied, kf, km, streams, cot, hid, weight)
+    )(fd, md, tied, kf, km, streams, cot, hid, cotangent, hot, weight)
     block_result_output = mm(block, order).astype(BF16)
     hidden_input_gradient = cotangent.astype(F32) + near + mm(far, turn)
 
-    embedding = jnp.stack(
-        [
-            jnp.sum(jnp.where(index[:, None] == b, hidden_input_gradient, 0.0), axis=0)
-            for b in range(4)
-        ]
-    )
-    small = jnp.concatenate([corr, embedding, jnp.zeros((3, width), F32)], axis=0)
-    summed = all_sum(small, count)
-
+    summed = summed.reshape(2, 32, width)
     all_turned = mm(swap(all_hidden), turn).astype(BF16)
     col_sg = col_sg.reshape(count * length, cw)
     other = swap(col_sg)
@@ -344,7 +308,9 @@
     dilated_kernel_gradient = jnp.concatenate(
         [a[7:12] + b[12:17], (b[7:12] + a[12:17])[:, ::-1]], axis=1
     )
-    embedding_table_gradient = jnp.concatenate([a[17:21], b[17:21]], axis=1)
+    embedding_table_gradient = jnp.concatenate(
+        [a[17:21] + a[21:25, ::-1], b[17:21] + b[21:25, ::-1]], axis=1
+    )
     return (
         block_result_output,
         hidden_input_gradient,

time: 130 us -> 127 us (0.977)
  Pallas kernels: 76.4 us -> 71.7 us
    pallas_call x1 -> x0, Pallas kernels: 21.2 us -> none  [all_sum(): pl.pallas_call(functools.partial(sum_kernel, count), out_shape=jax.ShapeD...]
    pallas_call x1, Pallas kernels: 55.2 us -> 71.7 us  [local(): pl.pallas_call(functools.partial(seq_kernel, count), out_shape=(jax.Shape...]
    rev x0 -> x2, local copies, waits for them, and re-layouts: none -> 1.42 us  [the longest x1 0.72 us: local(): b[21:25, ::-1]]
  transfers between devices with their start and end apart: 5 -> 5, of which waited for: 0 -> 1; matrix products, arithmetic and copies ran while one was open for 17% -> 19% of each run, Pallas kernels for 59% -> 57%
where the time goes in v3:
time: 127 us
  Pallas kernels  71.7 us (56%)
  matrix products  24.9 us (20%)
  between operations  14.3 us (11%)
  local copies, waits for them, and re-layouts  7.09 us (6%)
  other arithmetic  6.78 us (5%)
    pallas_call x1, Pallas kernels, local(): pl.pallas_call(functools.partial(seq_kernel, count), out_shape=(jax.Shape...  71.7 us
    dot_general x7, matrix products, mm(): return jnp.dot(a, b, preferred_element_type=F32)  13.5 us
    dot_general x1, matrix products, local(): lax.dot_general(all_turned, jnp.where(low, other, col_sg), rows, preferre...  6.57 us
    dot_general x1, matrix products, local(): lax.dot_general(all_hidden, jnp.where(low, col_sg, other), rows, preferre...  4.85 us
  transfers between devices with their start and end apart: 5, of which 1 were waited for; matrix products, arithmetic and copies ran while one was open for 19% of the time, Pallas kernels for 57%

profile of v3, /device:TPU:0, one launch (start us, length us, event | category | flops | bytes accessed | tf_op | source)
XLA Modules:
  0.0 126.6 jit_solution(18287503817017771253)
XLA Ops:
  7.2 0.7 broadcast_compare_fusion.3
  7.9 0.7 dynamic-slice_convert_fusion
  8.6 1.9 %add_convert_fusion.1 = bf16[128,1024]{1,0:T(8,128)(2,1)} fusion(bf16[128,1024]{1,0:T(8,128)(2,1)} %param.8, f32[1024]{0:T(1024)S(1)} %bitcast.68, f32[1024]{0:T(1024)S(1)} %bitcast.69, f32[1024]{0:T(1024)S(1)} %bitcast.70, f32[1024]{0:T(1024)S(1)} %bitcast.67, pred[128]{0:T(512)(128)(4,1)S(1)} %get-tuple-element.37, ...), kind=kLoop, calls=%fused_computation.27 | loop fusion | flops 1310720 | bytes 541184 | tf_op jit(solution)/shard_map/convert_element_type | solution.py:221
  10.5 0.5 collective-permute-start
  11.1 0.7 fusion.39.hot_ref
  11.7 0.7 slice.106
  12.5 0.8 fusion.47
  13.3 0.4 fusion.24
  13.8 5.7 %convolution_convert_fusion = bf16[128,4096]{1,0:T(8,128)(2,1)} fusion(bf16[1024,4096]{1,0:T(8,128)(2,1)} %w_ref.1, bf16[128,1024]{1,0:T(8,128)(2,1)S(1)} %fusion.24, bf16[128,1024]{1,0:T(8,128)(2,1)} %add_convert_fusion.1, pred[]{:T(512)S(6)} %eq.65), kind=kOutput, calls=%fused_computation | convolution fusion | flops 1074397184 | bytes 9961473 | tf_op jit(solution)/shard_map/dot_general | solution.py:23
  19.6 0.6 slice.110
  20.2 0.6 rev.24
  20.8 0.6 slice.113
  21.7 0.5 fusion.25.cot_ref
  22.1 0.4 fusion.18.hid_ref
  22.6 4.9 %add_convert_fusion.cur_ref = bf16[128,4096]{1,0:T(8,128)(2,1)S(1)} fusion(bf16[128,4096]{1,0:T(8,128)(2,1)S(1)} %collective-permute-done.1, bf16[1024,4096]{1,0:T(8,128)(2,1)} %w_ref.1, bf16[128,1024]{1,0:T(8,128)(2,1)S(1)} %copy-done.1, bf16[128,1024]{1,0:T(8,128)(2,1)S(1)} %fusion.24, pred[]{:T(512)S(6)} %eq.65), kind=kOutput, calls=%fused_computation.9 | convolution fusion | flops 1075445760 | bytes 11010049 | tf_op jit(solution)/shard_map/dot_general | solution.py:23
  27.6 0.6 slice-done.1
  28.1 71.7 %shard_map.127 = (bf16[128,1024]{1,0:T(8,128)(2,1)S(1)}, f32[2,32,8,128]{3,2,1,0:T(8,128)S(1)}, f32[128,1024]{1,0:T(8,128)S(1)}, bf16[128,1024]{1,0:T(8,128)(2,1)S(1)}, bf16[8,128,512]{2,1,0:T(8,128)(2,1)S(1)}) custom-call(s32[8]{0:T(128)S(1)} %get-tuple-element.33.fd_ref, s32[8]{0:T(128)S(1)} %get-tuple-element.32.md_ref, ...), custom_call_target="tpu_custom_call" | custom-call | flops 3000000000 | bytes 50000000 | tf_op jit(solution)/shard_map/pallas_call | solution.py:248
  99.9 0.2 rev.28
  100.1 0.7 rev.29
  100.8 0.7 rev.27
  101.6 0.7 rev.26
  102.3 0.5 collective-permute-start.2
  102.8 0.6 pad_maximum_fusion
  103.5 0.6 pad_maximum_fusion.2
  104.1 0.6 rev.30
  104.7 0.6 pad_maximum_fusion.1
  105.3 0.4 fusion.1
  105.7 0.9 add_add_fusion
  106.6 1.1 fusion.21
  107.8 0.6 collective-permute-done.3
  108.4 6.6 %fusion.4 = f32[1024,512]{1,0:T(8,128)} fusion(bf16[1024,1024]{1,0:T(8,128)(2,1)} %collective-permute-done.3, bf16[1024,512]{1,0:T(8,128)(2,1)} %collective-permute-done.2, bf16[1024,512]{1,0:T(8,128)(2,1)S(1)} %bitcast.62, pred[]{:T(512)S(6)} %eq.65), kind=kOutput, calls=%fused_computation.7 | convolution fusion | flops 3224895488 | bytes 6291457 | tf_op jit(solution)/shard_map/dot_general | solution.py:301
  114.9 4.8 %convolution_add_fusion = f32[1024,512]{1,0:T(8,128)} fusion(f32[1024,512]{1,0:T(8,128)} %fusion.4, bf16[1024,1024]{1,0:T(8,128)(2,1)} %all-gather.2.cloned.1.call-done, bf16[1024,512]{1,0:T(8,128)(2,1)S(1)} %bitcast.63, bf16[1024,512]{1,0:T(8,128)(2,1)} %collective-permute-done.2, pred[]{:T(512)S(6)} %eq.65), kind=kOutput, calls=%fused_computation.16 | convolution fusion | flops 1074790400 | bytes 8388609 | tf_op jit(solution)/shard_map/dot_general | solution.py:299
  (40 shorter events, 0.7 us)
Async XLA Ops:
  7.2 95.6 %all-gather.2.cloned.1.call-start = ((), (), s32[]{:S(2)}) async-start(), calls=%async_computation | async-start | bytes 2359296 | tf_op jit(solution)/shard_map/all_gather | solution.py:237
  10.5 2.8 %collective-permute-start = (bf16[128,1024]{1,0:T(8,128)(2,1)}, bf16[128,1024]{1,0:T(8,128)(2,1)S(1)}, u32[]{:S(2)}, u32[]{:S(2)}) collective-permute-start(bf16[128,1024]{1,0:T(8,128)(2,1)} %add_convert_fusion.1), channel_id=1, source_target_pairs={{0,1},{1,0},{2,3},{3,2},{4,5},{5,4},{6,7},{7,6},{8,9},{9,8},{10,11... | collective-permute-start | bytes 786440 | tf_op jit(solution)/shard_map/ppermute | solution.py:19
  13.7 5.9 %copy-start.4 = (s32[16]{0:T(128)S(1)}, s32[16]{0:T(128)}, u32[]{:S(2)}) copy-start(s32[16]{0:T(128)} %param.14) | copy-start | bytes 196
  13.7 7.1 %slice-start.2 = ((f32[5,2048]{1,0:T(8,128)}), f32[5,1024]{1,0:T(8,128)S(1)}, s32[]{:S(2)}) async-start(f32[5,2048]{1,0:T(8,128)} %param.13), calls=%async_computation.3 | async-start | bytes 65536 | tf_op jit(solution)/shard_map/slice | solution.py:231
  13.8 7.8 %copy-start.3 = (f32[5,2048]{1,0:T(8,128)S(1)}, f32[5,2048]{1,0:T(8,128)}, u32[]{:S(2)}) copy-start(f32[5,2048]{1,0:T(8,128)} %param.13) | copy-start | bytes 122884
  13.8 7.9 %copy-start.2 = (f32[7,2048]{1,0:T(8,128)S(1)}, f32[7,2048]{1,0:T(8,128)}, u32[]{:S(2)}) copy-start(f32[7,2048]{1,0:T(8,128)} %param.12) | copy-start | bytes 172036
  13.8 7.9 %copy-start = (bf16[128,1024]{1,0:T(8,128)(2,1)S(1)}, bf16[128,1024]{1,0:T(8,128)(2,1)}, u32[]{:S(2)}) copy-start(bf16[128,1024]{1,0:T(8,128)(2,1)} %cotn_ref.1) | copy-start | bytes 786436
  19.5 2.6 %copy-start.1 = (bf16[128,1024]{1,0:T(8,128)(2,1)S(1)}, bf16[128,1024]{1,0:T(8,128)(2,1)}, u32[]{:S(2)}) copy-start(bf16[128,1024]{1,0:T(8,128)(2,1)} %add_convert_fusion.1) | copy-start | bytes 786436
  19.5 3.1 %collective-permute-start.1 = (bf16[128,4096]{1,0:T(8,128)(2,1)}, bf16[128,4096]{1,0:T(8,128)(2,1)S(1)}, u32[]{:S(2)}, u32[]{:S(2)}) collective-permute-start(bf16[128,4096]{1,0:T(8,128)(2,1)} %convolution_convert_fusion), channel_id=1, source_target_pairs={{0,1},{1,0},{2,3},{3,2},{4,5},{5,4},{6,7},{7,6},{8,9},{9,8},{10,11... | collective-permute-start | bytes 3145736 | tf_op jit(solution)/shard_map/ppermute | solution.py:19
  22.1 5.4 %slice-start = ((s8[8388608]{0:T(1024)(128)(4,1)}), s8[4194304]{0:T(1024)(128)(4,1)S(1)}, s32[]{:S(2)}) async-start(s8[8388608]{0:T(1024)(128)(4,1)} %bitcast.59), calls=%async_computation.1 | async-start | bytes 8388608
  22.6 5.5 %slice-start.1 = ((s8[8388608]{0:T(1024)(128)(4,1)}), s8[4194304]{0:T(1024)(128)(4,1)S(1)}, s32[]{:S(2)}) async-start(s8[8388608]{0:T(1024)(128)(4,1)} %bitcast.59), calls=%async_computation.2 | async-start | bytes 8388608
  102.3 5.5 %collective-permute-start.2 = (bf16[1024,512]{1,0:T(8,128)(2,1)S(1)}, bf16[1024,512]{1,0:T(8,128)(2,1)}, u32[]{:S(2)}, u32[]{:S(2)}) collective-permute-start(bf16[1024,512]{1,0:T(8,128)(2,1)S(1)} %bitcast.61), channel_id=1, source_target_pairs={{0,1},{1,0},{2,3},{3,2},{4,5},{5,4},{6,7},{7,6},{8,9},{9,8},{10,11... | collective-permute-start | bytes 3145736 | tf_op jit(solution)/shard_map/ppermute | solution.py:19
  102.7 5.6 %collective-permute-start.3 = (bf16[1024,1024]{1,0:T(8,128)(2,1)}, bf16[1024,1024]{1,0:T(8,128)(2,1)}, u32[]{:S(2)}, u32[]{:S(2)}) collective-permute-start(bf16[1024,1024]{1,0:T(8,128)(2,1)} %all-gather.2.cloned.1.call-done), channel_id=1, source_target_pairs={{0,1},{1,0},{2,3},{3,2},{4,5},{5,4},{6,7},{7,6},{8,9},{9,8},{10,11... | collective-permute-start | bytes 6291464 | tf_op jit(solution)/shard_map/ppermute | solution.py:19
Sparse Core Ops, SparseCore 0:
  10.7 72.1 all-gather.1

commit v4 on v3

--- a/solution.py
+++ b/solution.py
@@ -238,8 +238,9 @@
 
     turned = mm(swap(hidden), turn).astype(BF16)
     hid = mm(hidden, order).astype(BF16)
-    far = mm(jnp.where(low, turned, hidden), weight).astype(BF16)
-    near = mm(jnp.where(low, hidden, turned), weight)
+    both = mm(jnp.concatenate([hidden, turned], axis=0), weight)
+    far = jnp.where(low, both[length:], both[:length]).astype(BF16)
+    near = jnp.where(low, both[:length], both[length:])
     streams = (near + swap(far).astype(F32)).astype(BF16)
 
     hot = (jnp.arange(16, dtype=jnp.int32)[:, None] == index[None, :]).astype(BF16)

time: 127 us -> 126 us (level)
  local copies, waits for them, and re-layouts: 7.09 us -> 11.9 us
  matrix products: 24.9 us -> 20.5 us
    unnamed x19 -> x27, local copies, waits for them, and re-layouts: 0.63 us -> 5.47 us
    dot_general x7 -> x6, matrix products: 13.5 us -> 9.56 us  [mm(): return jnp.dot(a, b, preferred_element_type=F32)]
  transfers between devices with their start and end apart: 5 -> 5, of which waited for: 1 -> 0; matrix products, arithmetic and copies ran while one was open for 19% -> 15% of each run, Pallas kernels for 57% -> 57%
where the time goes in v4:
time: 126 us
  Pallas kernels  71.3 us (57%)
  matrix products  20.5 us (16%)
  between operations  14.3 us (11%)
  local copies, waits for them, and re-layouts  11.9 us (9%)
  other arithmetic  5.75 us (5%)
  starting transfers between devices  1.66 us (1%)
    pallas_call x1, Pallas kernels, local(): pl.pallas_call(functools.partial(seq_kernel, count), out_shape=(jax.Shape...  71.3 us
    dot_general x6, matrix products, mm(): return jnp.dot(a, b, preferred_element_type=F32)  9.56 us
    dot_general x1, matrix products, local(): lax.dot_general(all_turned, jnp.where(low, other, col_sg), rows, preferre...  6.73 us
    unnamed x27, local copies, waits for them, and re-layouts  5.47 us
    dot_general x1, matrix products, local(): lax.dot_general(all_hidden, jnp.where(low, col_sg, other), rows, preferre...  4.22 us
  transfers between devices with their start and end apart: 5, of which 0 were waited for; matrix products, arithmetic and copies ran while one was open for 15% of the time, Pallas kernels for 57%

profile of v4, /device:TPU:0, one launch (start us, length us, event | category | flops | bytes accessed | tf_op | source)
XLA Modules:
  0.0 125.5 jit_solution(11955843353440001626)
XLA Ops:
  7.2 0.7 dynamic-slice_convert_fusion
  7.9 0.7 broadcast_compare_fusion.3
  8.6 1.2 add_convert_fusion.1
  9.8 0.5 collective-permute-start
  10.5 0.7 fusion.36.hot_ref
  11.2 0.7 slice.114
  12.0 0.8 fusion.45
  12.8 0.4 fusion.24
  13.3 5.9 %fusion.32 = f32[256,4096]{1,0:T(8,128)S(1)} fusion(bf16[1024,4096]{1,0:T(8,128)(2,1)} %w_ref.1, bf16[128,1024]{1,0:T(8,128)(2,1)S(1)} %fusion.24, bf16[128,1024]{1,0:T(8,128)(2,1)} %copy-done.3), kind=kOutput, calls=%fused_computation.26 | convolution fusion | flops 2148532224 | bytes 13107200 | tf_op jit(solution)/shard_map/dot_general | solution.py:23
  19.4 1.8 %copy-done.1 = f32[256,4096]{1,0:T(8,128)} copy-done((f32[256,4096]{1,0:T(8,128)}, f32[256,4096]{1,0:T(8,128)S(1)}, u32[]{:S(2)}) %copy-start.1) | copy-done | bytes 4194328
  21.1 0.5 collective-permute-start.1
  21.6 0.6 slice.118
  22.2 0.6 rev.24
  23.0 0.6 slice.121
  23.7 0.5 fusion.25.cot_ref
  24.2 0.4 fusion.18.hid_ref
  24.6 1.2 copy-done.2
  26.2 0.9 slice-done
  27.1 1.3 %slice-done.1 = s8[4194304]{0:T(1024)(128)(4,1)S(1)} async-done(((s8[8388608]{0:T(1024)(128)(4,1)}), s8[4194304]{0:T(1024)(128)(4,1)S(1)}, s32[]{:S(2)}) %slice-start.1) | async-done | bytes 4194328
  28.5 71.3 %shard_map.127 = (bf16[128,1024]{1,0:T(8,128)(2,1)S(1)}, f32[2,32,8,128]{3,2,1,0:T(8,128)S(1)}, f32[128,1024]{1,0:T(8,128)S(1)}, bf16[128,1024]{1,0:T(8,128)(2,1)S(1)}, bf16[8,128,512]{2,1,0:T(8,128)(2,1)S(1)}) custom-call(s32[8]{0:T(128)S(1)} %get-tuple-element.33.fd_ref, s32[8]{0:T(128)S(1)} %get-tuple-element.32.md_ref, ...), custom_call_target="tpu_custom_call" | custom-call | flops 3000000000 | bytes 50000000 | tf_op jit(solution)/shard_map/pallas_call | solution.py:249
  99.8 0.5 collective-permute-start.2
  100.4 0.7 rev.27
  101.1 0.7 rev.26
  102.2 0.6 pad_maximum_fusion.2
  102.8 0.6 rev.29
  103.5 0.6 rev.30
  104.1 0.6 pad_maximum_fusion
  104.7 0.6 pad_maximum_fusion.1
  105.3 1.2 add_add_fusion
  106.6 1.1 fusion.21
  107.7 6.7 %fusion.4 = f32[1024,512]{1,0:T(8,128)} fusion(bf16[1024,1024]{1,0:T(8,128)(2,1)} %collective-permute-done.3, bf16[1024,512]{1,0:T(8,128)(2,1)} %collective-permute-done.2, bf16[1024,512]{1,0:T(8,128)(2,1)S(1)} %bitcast.61, pred[]{:T(512)S(6)} %eq.65), kind=kOutput, calls=%fused_computation.6 | convolution fusion | flops 3224895488 | bytes 6291457 | tf_op jit(solution)/shard_map/dot_general | solution.py:302
  114.5 4.2 %convolution_add_fusion = f32[1024,512]{1,0:T(8,128)} fusion(f32[1024,512]{1,0:T(8,128)} %fusion.4, bf16[1024,1024]{1,0:T(8,128)(2,1)S(1)} %copy-done.8, bf16[1024,512]{1,0:T(8,128)(2,1)S(1)} %bitcast.62, bf16[1024,512]{1,0:T(8,128)(2,1)} %collective-permute-done.2, pred[]{:T(512)S(6)} %eq.65), kind=kOutput, calls=%fused_computation.16 | convolution fusion | flops 1074790400 | bytes 8388609 | tf_op jit(solution)/shard_map/dot_general | solution.py:300
  (48 shorter events, 1.6 us)
Async XLA Ops:
  7.2 94.9 %all-gather.2.cloned.1.call-start = ((), (), s32[]{:S(2)}) async-start(), calls=%async_computation | async-start | bytes 2359296 | tf_op jit(solution)/shard_map/all_gather | solution.py:237
  9.8 0.7 copy-start.3
  9.8 3.0 %collective-permute-start = (bf16[128,1024]{1,0:T(8,128)(2,1)S(1)}, bf16[128,1024]{1,0:T(8,128)(2,1)S(1)}, u32[]{:S(2)}, u32[]{:S(2)}) collective-permute-start(bf16[128,1024]{1,0:T(8,128)(2,1)S(1)} %add_convert_fusion.1), channel_id=1, source_target_pairs={{0,1},{1,0},{2,3},{3,2},{4,5},{5,4},{6,7},{7,6},{8,9},{9,8},{10,11... | collective-permute-start | bytes 786440 | tf_op jit(solution)/shard_map/ppermute | solution.py:19
  13.2 8.4 %copy-start.7 = (s32[16]{0:T(128)S(1)}, s32[16]{0:T(128)}, u32[]{:S(2)}) copy-start(s32[16]{0:T(128)} %param.14) | copy-start | bytes 196
  13.3 9.8 %slice-start.2 = ((f32[5,2048]{1,0:T(8,128)}), f32[5,1024]{1,0:T(8,128)S(1)}, s32[]{:S(2)}) async-start(f32[5,2048]{1,0:T(8,128)} %param.13), calls=%async_computation.3 | async-start | bytes 65536 | tf_op jit(solution)/shard_map/slice | solution.py:231
  13.3 10.3 %copy-start.6 = (f32[5,2048]{1,0:T(8,128)S(1)}, f32[5,2048]{1,0:T(8,128)}, u32[]{:S(2)}) copy-start(f32[5,2048]{1,0:T(8,128)} %param.13) | copy-start | bytes 122884
  13.3 10.3 %copy-start.5 = (f32[7,2048]{1,0:T(8,128)S(1)}, f32[7,2048]{1,0:T(8,128)}, u32[]{:S(2)}) copy-start(f32[7,2048]{1,0:T(8,128)} %param.12) | copy-start | bytes 172036
  13.3 10.4 %copy-start = (bf16[128,1024]{1,0:T(8,128)(2,1)S(1)}, bf16[128,1024]{1,0:T(8,128)(2,1)}, u32[]{:S(2)}) copy-start(bf16[128,1024]{1,0:T(8,128)(2,1)} %cotn_ref.1) | copy-start | bytes 786436
  19.2 2.0 %copy-start.1 = (f32[256,4096]{1,0:T(8,128)}, f32[256,4096]{1,0:T(8,128)S(1)}, u32[]{:S(2)}) copy-start(f32[256,4096]{1,0:T(8,128)S(1)} %fusion.32) | copy-start | bytes 12582916
  19.2 5.0 %copy-start.4 = (bf16[128,1024]{1,0:T(8,128)(2,1)S(1)}, bf16[128,1024]{1,0:T(8,128)(2,1)}, u32[]{:S(2)}) copy-start(bf16[128,1024]{1,0:T(8,128)(2,1)} %copy-done.3) | copy-start | bytes 786436
  21.1 3.5 %collective-permute-start.1 = (bf16[128,4096]{1,0:T(8,128)(2,1)S(1)}, bf16[128,4096]{1,0:T(8,128)(2,1)S(1)}, u32[]{:S(2)}, u32[]{:S(2)}) collective-permute-start(bf16[128,4096]{1,0:T(8,128)(2,1)S(1)} %select_convert_fusion), channel_id=1, source_target_pairs={{0,1},{1,0},{2,3},{3,2},{4,5},{5,4},{6,7},{7,6},{8,9},{9,8},{10,11... | collective-permute-start | bytes 3145736 | tf_op jit(solution)/shard_map/ppermute | solution.py:19
  23.7 2.2 %copy-start.2 = (f32[256,4096]{1,0:T(8,128)S(1)}, f32[256,4096]{1,0:T(8,128)}, u32[]{:S(2)}) copy-start(f32[256,4096]{1,0:T(8,128)} %copy-done.1) | copy-start | bytes 12582916
  23.7 3.5 %slice-start = ((s8[8388608]{0:T(1024)(128)(4,1)}), s8[4194304]{0:T(1024)(128)(4,1)S(1)}, s32[]{:S(2)}) async-start(s8[8388608]{0:T(1024)(128)(4,1)} %bitcast.58), calls=%async_computation.1 | async-start | bytes 8388608
  24.2 4.3 %slice-start.1 = ((s8[8388608]{0:T(1024)(128)(4,1)}), s8[4194304]{0:T(1024)(128)(4,1)S(1)}, s32[]{:S(2)}) async-start(s8[8388608]{0:T(1024)(128)(4,1)} %bitcast.58), calls=%async_computation.2 | async-start | bytes 8388608
  99.8 7.9 %collective-permute-start.2 = (bf16[1024,512]{1,0:T(8,128)(2,1)S(1)}, bf16[1024,512]{1,0:T(8,128)(2,1)}, u32[]{:S(2)}, u32[]{:S(2)}) collective-permute-start(bf16[1024,512]{1,0:T(8,128)(2,1)S(1)} %bitcast.60), channel_id=1, source_target_pairs={{0,1},{1,0},{2,3},{3,2},{4,5},{5,4},{6,7},{7,6},{8,9},{9,8},{10,11... | collective-permute-start | bytes 3145736 | tf_op jit(solution)/shard_map/ppermute | solution.py:19
  102.0 5.7 %collective-permute-start.3 = (bf16[1024,1024]{1,0:T(8,128)(2,1)}, bf16[1024,1024]{1,0:T(8,128)(2,1)}, u32[]{:S(2)}, u32[]{:S(2)}) collective-permute-start(bf16[1024,1024]{1,0:T(8,128)(2,1)} %all-gather.2.cloned.1.call-done), channel_id=1, source_target_pairs={{0,1},{1,0},{2,3},{3,2},{4,5},{5,4},{6,7},{7,6},{8,9},{9,8},{10,11... | collective-permute-start | bytes 6291464 | tf_op jit(solution)/shard_map/ppermute | solution.py:19
  107.7 6.7 %copy-start.8 = (bf16[1024,1024]{1,0:T(8,128)(2,1)S(1)}, bf16[1024,1024]{1,0:T(8,128)(2,1)}, u32[]{:S(2)}) copy-start(bf16[1024,1024]{1,0:T(8,128)(2,1)} %all-gather.2.cloned.1.call-done) | copy-start | bytes 6291460
Sparse Core Ops, SparseCore 0:
  10.7 71.8 all-gather.1
